TPU v7x, 256 devices: a whole 4x4x8 slice. The times are simulated.
256 devices in a mesh: tp: 8 (over y, core), row: 4 (over x), kv: 8 (over z).
Axes of the slice: x: 4, y: 4, z: 8, core: 2. Of those that a mesh axis runs over, the one named last changes fastest.
Arguments:
- tokens: bfloat16 [32, 8192], P(None, ('row', 'kv')), may hold values from -5 to 5
- attn_gain: bfloat16 [8192], P(('row', 'kv')), may hold values from 0.099609375 to 1.8984375
- w_qkv: bfloat16 [8192, 10240], P(('row', 'kv'), 'tp'), may hold values from -0.0625 to 0.0625
- w_out: bfloat16 [8192, 8192], P('tp', ('row', 'kv')), may hold values from -0.0625 to 0.0625
- ffn_gain: bfloat16 [8192], P(('row', 'kv')), may hold values from 0.099609375 to 1.8984375
- w_gate: bfloat16 [8192, 14336], P(('row', 'kv'), 'tp'), may hold values from -0.0625 to 0.0625
- w_up: bfloat16 [8192, 14336], P(('row', 'kv'), 'tp'), may hold values from -0.0625 to 0.0625
- w_down: bfloat16 [14336, 8192], P('tp', ('row', 'kv')), may hold values from -0.09375 to 0.09375
- cache_keys: bfloat16 [32, 16384, 1024], P('row', 'kv', 'tp'), may hold values from -94 to 94
- cache_values: bfloat16 [32, 16384, 1024], P('row', 'kv', 'tp'), may hold values from -10 to 10
- cache_len: int32 [32], replicated, may hold values from 1 to 16383, 209715 in all
- pool_seq: int32 [32], replicated, may hold values from 0 to 31, each once
Outputs:
- layer_out: bfloat16 [32, 8192], P(None, ('row', 'kv'))
- new_keys: bfloat16 [32, 1024], P('row', 'tp')
- new_values: bfloat16 [32, 1024], P('row', 'tp')
Inputs may be any that keep to these rules, and one draw needn't show every extreme that they name: `cache_len`: cache lengths of the sequences; they sum to 209715 and the largest is exactly 16383. `pool_seq`: each sequence stands in exactly one pool slot.
All inputs are finite; a program needn't handle non-finite values.
Results may differ from a plain program's by a relative error of at most 0.02.
Values may be sent and summed in bfloat16 or wider, within the bound.
A program may use at most 64 MiB of HBM per device.

v0:
```python
import jax
import jax.numpy as jnp
from jax import lax
from jax.sharding import PartitionSpec as P

D = 8192
HEAD = 128
GROUP = 8


epsilon = 1e-05
rope_base = 500000.0
floor_score = -1e30


def combined_all(value, axis, join):
    pieces = jax.tree.map(lambda part: lax.all_gather(part, axis), value)
    head = jax.tree.map(lambda part: part[0], pieces)
    tail = jax.tree.map(lambda part: part[1:], pieces)
    running, _ = lax.scan(lambda running, piece: (join(running, piece), None), head, tail)
    return running


def rotate(vectors, positions):
    half_width = vectors.shape[-1] // 2
    frequency = rope_base ** (
        -(jnp.arange(half_width, dtype=jnp.float32) * 2.0 / vectors.shape[-1])
    )
    angles = positions.astype(jnp.float32)[:, None] * frequency[None, :]
    cosine = jnp.cos(angles)[:, None, :]
    sine_part = jnp.sin(angles)[:, None, :]
    first_half = vectors[..., :half_width]
    second_half = vectors[..., half_width:]
    return jnp.concatenate(
        [
            first_half * cosine - second_half * sine_part,
            second_half * cosine + first_half * sine_part,
        ],
        axis=-1,
    )


def fold_scores(scores, allowed, values_part, carried):
    old_peak, old_sum, old_numer = carried
    new_peak = jnp.maximum(old_peak, jnp.max(jnp.where(allowed, scores, floor_score), axis=-1))
    weights = jnp.where(allowed, jnp.exp(scores - new_peak[..., None]), 0.0)
    faded = jnp.exp(old_peak - new_peak)
    new_sum = old_sum * faded + jnp.sum(weights, axis=-1)
    product = jnp.einsum(
        "sgqt,stgd->sgqd",
        weights.astype(jnp.bfloat16),
        values_part,
        preferred_element_type=jnp.float32,
    )
    return (new_peak, new_sum, old_numer * faded[..., None] + product)


def attend_cache(
    queries, keys_local, values_local, limits, offset, span_width, span_count, carried
):
    slot_count = keys_local.shape[0]
    groups = queries.shape[1]
    score_scale = queries.shape[-1] ** (-0.5)

    def one_span(span_index, state_now):
        span_start = span_index * span_width
        keys_part = keys_local.reshape(slot_count, span_width, groups, -1)
        values_part = values_local.reshape(slot_count, span_width, groups, -1)
        positions = offset + span_start + jnp.arange(span_width, dtype=jnp.int32)
        allowed = (positions[None, :] < limits[:, None])[:, None, None, :]
        scores = (
            jnp.einsum("sgqd,stgd->sgqt", queries, keys_part, preferred_element_type=jnp.float32)
            * score_scale
        )
        return fold_scores(scores, allowed, values_part, state_now)

    return lax.fori_loop(0, span_count, one_span, carried)


def combine_parts(first_part, second_part):
    joint_peak = jnp.maximum(first_part[0], second_part[0])
    first_fade = jnp.exp(first_part[0] - joint_peak)
    second_fade = jnp.exp(second_part[0] - joint_peak)
    joint_sum = first_part[1] * first_fade + second_part[1] * second_fade
    joint_numer = first_part[2] * first_fade[..., None] + second_part[2] * second_fade[..., None]
    return (joint_peak, joint_sum, joint_numer)


def finish_rows(parts):
    normalized = parts[2] / parts[1][..., None]
    return normalized.astype(jnp.bfloat16).reshape(parts[2].shape[0], -1)


def local(
    tokens,
    attn_gain,
    w_qkv,
    w_out,
    ffn_gain,
    w_gate,
    w_up,
    w_down,
    cache_keys,
    cache_values,
    cache_len,
    pool_seq,
):
    seq_count = tokens.shape[0]
    stream = tokens.astype(jnp.float32)
    first_sum = lax.psum(jnp.sum(stream * stream, axis=1), ("row", "kv"))
    normed = (
        stream * lax.rsqrt(first_sum / D + epsilon)[:, None] * attn_gain.astype(jnp.float32)
    ).astype(jnp.bfloat16)
    ordered = jnp.take(normed, pool_seq, axis=0)
    group_rows = seq_count // lax.axis_size("row")
    united_rows = lax.psum_scatter(
        jnp.dot(ordered, w_qkv, preferred_element_type=jnp.float32),
        "row",
        scatter_dimension=0,
        tiled=True,
    )
    united_rows = lax.psum(united_rows, "kv")
    groups = united_rows.shape[1] // ((GROUP + 2) * HEAD)
    united_rows = united_rows.reshape(group_rows, groups, GROUP + 2, HEAD)
    slot_ids = lax.axis_index("row") * group_rows + jnp.arange(group_rows, dtype=jnp.int32)
    limits = jnp.take(cache_len, jnp.take(pool_seq, slot_ids))
    queries = rotate(united_rows[:, :, :GROUP].reshape(group_rows, groups * GROUP, HEAD), limits)
    queries = queries.astype(jnp.bfloat16).reshape(group_rows, groups, GROUP, HEAD)
    key_new = rotate(united_rows[:, :, GROUP], limits).astype(jnp.bfloat16)
    value_new = united_rows[:, :, GROUP + 1].astype(jnp.bfloat16)
    block_len = cache_keys.shape[1]
    offset = lax.axis_index("kv") * block_len
    start_state = (
        jnp.full((group_rows, groups, GROUP), floor_score, jnp.float32),
        jnp.zeros((group_rows, groups, GROUP), jnp.float32),
        jnp.zeros((group_rows, groups, GROUP, HEAD), jnp.float32),
    )
    span_count = 1
    carried = attend_cache(
        queries, cache_keys, cache_values, limits, offset, block_len, span_count, start_state
    )
    owns_new = limits // block_len == lax.axis_index("kv")
    fresh_scores = jnp.einsum(
        "sgqd,sgd->sgq", queries, key_new, preferred_element_type=jnp.float32
    )[..., None] * HEAD ** (-0.5)
    carried = fold_scores(fresh_scores, owns_new[:, None, None, None], value_new[:, None], carried)
    joined = combined_all((carried[0], carried[1], carried[2]), "kv", combine_parts)
    mixed_rows = finish_rows(joined)
    projected = jnp.dot(
        lax.all_gather(mixed_rows, "row", axis=0, tiled=True),
        w_out,
        preferred_element_type=jnp.float32,
    )
    slot_of = (
        jnp.zeros((seq_count,), jnp.int32).at[pool_seq].set(jnp.arange(seq_count, dtype=jnp.int32))
    )
    projected = jnp.take(projected, slot_of, axis=0)
    projected = lax.psum(projected, "tp")
    stream_two = (stream + projected).astype(jnp.bfloat16)
    stream_wide = stream_two.astype(jnp.float32)
    second_sum = lax.psum(jnp.sum(stream_wide * stream_wide, axis=1), ("row", "kv"))
    normed_two = (
        stream_wide * lax.rsqrt(second_sum / D + epsilon)[:, None] * ffn_gain.astype(jnp.float32)
    ).astype(jnp.bfloat16)
    gate_sum, up_sum = lax.psum(
        (
            jnp.dot(normed_two, w_gate, preferred_element_type=jnp.float32),
            jnp.dot(normed_two, w_up, preferred_element_type=jnp.float32),
        ),
        ("row", "kv"),
    )
    activated = (jax.nn.silu(gate_sum) * up_sum).astype(jnp.bfloat16)
    down_sum = jnp.dot(activated, w_down, preferred_element_type=jnp.float32)
    down_sum = lax.psum(down_sum, "tp")
    layer_out = (stream_wide + down_sum).astype(jnp.bfloat16)
    return (layer_out, key_new.reshape(group_rows, -1), value_new.reshape(group_rows, -1))


def solution(mesh):
    return jax.shard_map(
        local,
        mesh=mesh,
        in_specs=(
            P(None, ("row", "kv")),
            P(("row", "kv")),
            P(("row", "kv"), "tp"),
            P("tp", ("row", "kv")),
            P(("row", "kv")),
            P(("row", "kv"), "tp"),
            P(("row", "kv"), "tp"),
            P("tp", ("row", "kv")),
            P("row", "kv", "tp"),
            P("row", "kv", "tp"),
            P(),
            P(),
        ),
        out_specs=(P(None, ("row", "kv")), P("row", "tp"), P("row", "tp")),
        check_vma=False,
    )
```

profile of v0, /device:TPU:1, one launch (start us, length us, event | category | flops | bytes accessed | tf_op | source)
XLA Modules:
  0.0 500.0 jit_solution(5004761198493843408)
XLA Ops:
  7.2 0.7 compare_select_fusion.3
  8.0 0.7 compare_and_fusion
  8.6 0.8 fusion.15
  9.4 64.3 %psum.49 = f32[32]{0:T(128)S(1)} all-reduce(f32[32]{0:T(128)S(1)} %fusion.15), channel_id=1, replica_groups=mesh['tp'=8,'row'=4,'kv'=8] {'row','kv'}, use_global_device_ids=true, to_apply=%region_2.0 | all-reduce | flops 32 | bytes 256 | tf_op jit(solution)/shard_map/psum | solution.py:110
  73.8 0.7 convert_element_type.61
  74.5 0.8 fusion.17
  75.3 0.6 gather_fusion
  75.9 2.0 fusion.23
  78.0 0.7 scatter_custom_fusion
  78.7 0.7 convert_element_type.70
  79.4 1.3 gather_fusion.2
  80.7 1.3 gather_fusion.3
  82.3 24.6 %reduce-scatter.2.cloned.1.call-done = f32[8,1280]{1,0:T(8,128)} async-done(((f32[32,1280]{1,0:T(8,128)}), f32[8,1280]{1,0:T(8,128)}) %reduce-scatter.2.cloned.1.call-update) | async-done | bytes 40976 | tf_op jit(solution)/shard_map/reduce_scatter | solution.py:116
  106.9 0.8 copy.25
  107.7 23.4 %psum.50 = f32[8,1,10,128]{3,2,0,1:T(8,128)S(1)} all-reduce(f32[8,1,10,128]{3,2,0,1:T(8,128)S(1)} %copy.25), channel_id=1, replica_groups=mesh['tp'=8,'row'=4,'kv'=8] {'kv'}, use_global_device_ids=true, to_apply=%region_4.6 | all-reduce | flops 10240 | bytes 81920 | tf_op jit(solution)/shard_map/psum | solution.py:122
  131.6 3.8 select_reduce_fusion
  135.5 18.2 %all-gather = f32[64,8]{1,0:T(8,128)S(1)} all-gather(f32[8,8]{1,0:T(8,128)S(1)} %get-tuple-element.116), channel_id=2, replica_groups=mesh['tp'=8,'row'=4,'kv'=8] {'kv'}, dimensions={0}, use_global_device_ids=true | all-gather | bytes 2304 | tf_op jit(solution)/shard_map/all_gather | solution.py:17
  154.0 18.1 %all-gather.1 = f32[64,8]{1,0:T(8,128)S(1)} all-gather(f32[8,8]{1,0:T(8,128)S(1)} %get-tuple-element.126), channel_id=3, replica_groups=mesh['tp'=8,'row'=4,'kv'=8] {'kv'}, dimensions={0}, use_global_device_ids=true | all-gather | bytes 2304 | tf_op jit(solution)/shard_map/all_gather | solution.py:17
  172.7 0.7 fusion.6
  173.5 18.9 %all-gather.2 = f32[64,8,128]{2,1,0:T(8,128)S(1)} all-gather(f32[8,8,128]{2,1,0:T(8,128)S(1)} %fusion.6), channel_id=4, replica_groups=mesh['tp'=8,'row'=4,'kv'=8] {'kv'}, dimensions={0}, use_global_device_ids=true | all-gather | bytes 294912 | tf_op jit(solution)/shard_map/all_gather | solution.py:17
  192.4 1.1 while.2
  193.6 9.0 %all_gather.21 = bf16[32,1024]{1,0:T(8,128)(2,1)S(1)} all-gather(bf16[8,1024]{1,0:T(8,128)(2,1)S(1)} %bitcast.82), channel_id=1, replica_groups=mesh['tp'=8,'row'=4,'kv'=8] {'row'}, dimensions={0}, use_global_device_ids=true | all-gather | bytes 81920 | tf_op jit(solution)/shard_map/all_gather | solution.py:150
  202.8 0.6 gather_fusion.1
  203.5 51.7 %psum.51 = f32[32,256]{1,0:T(8,128)S(1)} all-reduce(f32[32,256]{1,0:T(8,128)S(1)} %broadcast_select_fusion), channel_id=1, replica_groups=mesh['tp'=8,'row'=4,'kv'=8] {'tp'}, use_global_device_ids=true, to_apply=%region_9.11 | all-reduce | flops 8192 | bytes 65536 | tf_op jit(solution)/shard_map/psum | solution.py:158
  255.3 56.9 %psum.52 = f32[32]{0:T(128)S(1)} all-reduce(f32[32]{0:T(128)S(1)} %get-tuple-element.113), channel_id=1, replica_groups=mesh['tp'=8,'row'=4,'kv'=8] {'row','kv'}, use_global_device_ids=true, to_apply=%region_11.13 | all-reduce | flops 32 | bytes 256 | tf_op jit(solution)/shard_map/psum | solution.py:161
  312.2 1.0 fusion.38
  313.2 1.0 fusion.40
  314.3 0.7 pad_maximum_fusion.3
  314.9 150.5 %all-reduce.3.cloned.1.call-done = (f32[32,1792]{1,0:T(8,128)}, f32[32,1792]{1,0:T(8,128)}) async-done(((f32[32,1792]{1,0:T(8,128)}, f32[32,1792]{1,0:T(8,128)}), (f32[32,1792]{1,0:T(8,128)}, f32[32,1792]{1,0:T(8,128)})) %all-reduce.3.cloned.1.call-update) | async-done | bytes 458768 | tf_op jit(solution)/shard_map/psum | solution.py:165
  465.4 1.7 fusion.13
  467.1 25.5 %psum.55 = f32[32,256]{1,0:T(8,128)S(1)} all-reduce(f32[32,256]{1,0:T(8,128)S(1)} %fusion.13), channel_id=1, replica_groups=mesh['tp'=8,'row'=4,'kv'=8] {'tp'}, use_global_device_ids=true, to_apply=%region_14.16 | all-reduce | flops 8192 | bytes 65536 | tf_op jit(solution)/shard_map/psum | solution.py:174
  492.5 0.6 fusion.22
  (81 shorter events, 3.3 us)
Async XLA Ops:
  7.2 305.0 %copy-start = (bf16[256,1792]{1,0:T(8,128)(2,1)S(1)}, bf16[256,1792]{1,0:T(8,128)(2,1)}, u32[]{:S(2)}) copy-start(bf16[256,1792]{1,0:T(8,128)(2,1)} %param.22) | copy-start | bytes 2752516
  7.2 99.7 %reduce-scatter.2.cloned.1.call-start = ((), (), s32[]{:S(2)}) async-start(), calls=%async_computation.1 | async-start | bytes 204800 | tf_op jit(solution)/shard_map/reduce_scatter | solution.py:116
  77.9 387.5 %all-reduce.3.cloned.1.call-start = ((), (), s32[]{:S(2)}) async-start(), calls=%async_computation.2 | async-start | bytes 917504 | tf_op jit(solution)/shard_map/psum | solution.py:165
  131.1 41.6 %copy-start.1 = (bf16[8,2048,128]{2,1,0:T(8,128)(2,1)S(1)}, bf16[8,2048,128]{2,1,0:T(8,128)(2,1)}, u32[]{:S(2)}) copy-start(bf16[8,2048,128]{2,1,0:T(8,128)(2,1)} %param.25) | copy-start | bytes 12582916
  135.4 67.2 %copy-start.3 = (bf16[1024,256]{1,0:T(8,128)(2,1)S(1)}, bf16[1024,256]{1,0:T(8,128)(2,1)}, u32[]{:S(2)}) copy-start(bf16[1024,256]{1,0:T(8,128)(2,1)} %param.19) | copy-start | bytes 1572868
  153.7 101.5 %copy-start.4 = (bf16[32,256]{1,0:T(8,128)(2,1)S(1)}, bf16[32,256]{1,0:T(8,128)(2,1)}, u32[]{:S(2)}) copy-start(bf16[32,256]{1,0:T(8,128)(2,1)} %param.16) | copy-start | bytes 49156
  172.7 140.5 %copy-start.2 = (bf16[256,1792]{1,0:T(8,128)(2,1)S(1)}, bf16[256,1792]{1,0:T(8,128)(2,1)}, u32[]{:S(2)}) copy-start(bf16[256,1792]{1,0:T(8,128)(2,1)} %param.21) | copy-start | bytes 2752516
Sparse Core Ops, SparseCore 0:
  78.1 28.7 reduce-scatter.1
  314.4 150.9 all-reduce.2
where the time goes:
time: 501 us; the launch traced here: 500 us
  blocking collectives  286 us (57%)
  waiting for transfers between devices  175 us (35%)
  between operations  14.3 us (3%)
  matrix products  10.6 us (2%)
  other arithmetic  8.26 us (2%)
  local copies, waits for them, and re-layouts  5.39 us (1%)
    psum x1, waiting for transfers between devices, local(): lax.psum((jnp.dot(normed_two, w_gate, preferred_element_type=jnp.float32)...  151 us
    psum x1, blocking collectives, local(): first_sum = lax.psum(jnp.sum(stream * stream, axis=1), ('row', 'kv'))  64.3 us
    psum x1, blocking collectives, local(): lax.psum(jnp.sum(stream_wide * stream_wide, axis=1), ('row', 'kv'))  56.9 us
    all_gather x3, blocking collectives, combined_all(): pieces = jax.tree.map(lambda part: lax.all_gather(part, axis), value)  55.2 us
    psum x1, blocking collectives, local(): projected = lax.psum(projected, 'tp')  51.7 us
    psum x1, blocking collectives, local(): down_sum = lax.psum(down_sum, 'tp')  25.5 us
    reduce_scatter x1, waiting for transfers between devices, local(): lax.psum_scatter(jnp.dot(ordered, w_qkv, preferred_element_type=jnp.float...  24.6 us
    psum x1, blocking collectives, local(): united_rows = lax.psum(united_rows, 'kv')  23.4 us
  transfers between devices with their start and end apart: 2, of which 2 were waited for; matrix products, arithmetic and copies ran while one was open for 1% of the time, Pallas kernels for 0%

commit v1 on v0

v1 whole, which is shorter than its diff:
```python
import functools

import jax
import jax.numpy as jnp
from jax import lax
from jax.experimental import pallas as pl
from jax.experimental.pallas import tpu as pltpu
from jax.sharding import PartitionSpec as P

D = 8192
HEAD = 128
GROUP = 8
EPSILON = 1e-05
ROPE_BASE = 500000.0
FLOOR = -1e30
MESH = pl.DeviceIdType.MESH
F32 = jnp.float32
BF16 = jnp.bfloat16


def iota(shape, dim):
    return lax.broadcasted_iota(jnp.int32, shape, dim)


def kernel(
    tp_size,
    row_size,
    kv_size,
    pool_smem,
    len_smem,
    pool_row,
    tokens,
    gains,
    cosines,
    sines,
    w_qkv,
    w_out,
    w_gate,
    w_up,
    w_down,
    cache_keys,
    cache_values,
    layer_out,
    new_keys,
    new_values,
    qkv_v,
    out_v,
    gate_v,
    up_v,
    down_v,
    keys_v,
    values_v,
    s1,
    r1,
    s2,
    r2,
    s3,
    r3,
    s4,
    r4,
    s5,
    r5,
    s6,
    r6,
    w7,
    s7,
    r7,
    s8,
    r8,
    w8,
    s9,
    r9,
    load_sems,
    send_sems,
    recv_sems,
):
    plane = row_size * kv_size
    tp = lax.axis_index("tp")
    row = lax.axis_index("row")
    kv = lax.axis_index("kv")
    me = row * kv_size + kv

    barrier = pltpu.get_barrier_semaphore()

    def greet_plane(step, carry):
        other = lax.rem(me + step, plane)
        pl.semaphore_signal(
            barrier,
            inc=1,
            device_id={"row": other // kv_size, "kv": lax.rem(other, kv_size)},
            device_id_type=MESH,
        )
        return carry

    def greet_tp(step, carry):
        pl.semaphore_signal(
            barrier, inc=1, device_id={"tp": lax.rem(tp + step, tp_size)}, device_id_type=MESH
        )
        return carry

    lax.fori_loop(1, plane, greet_plane, 0)
    lax.fori_loop(1, tp_size, greet_tp, 0)

    loads = []
    for index, (source, target) in enumerate(
        (
            (w_qkv, qkv_v),
            (cache_keys, keys_v),
            (cache_values, values_v),
            (w_out, out_v),
            (w_gate, gate_v),
            (w_up, up_v),
            (w_down, down_v),
        )
    ):
        load = pltpu.make_async_copy(source, target, load_sems.at[index])
        load.start()
        loads.append(load)

    def send_plane(phase, source, target):
        def one(step, carry):
            other = lax.rem(me + step, plane)
            pltpu.make_async_remote_copy(
                src_ref=source(other),
                dst_ref=target,
                send_sem=send_sems.at[phase],
                recv_sem=recv_sems.at[phase],
                device_id={"row": other // kv_size, "kv": lax.rem(other, kv_size)},
                device_id_type=MESH,
            ).start()
            return carry

        lax.fori_loop(1, plane, one, 0)

    def send_kv(phase, source, target):
        def one(step, carry):
            other = lax.rem(kv + step, kv_size)
            pltpu.make_async_remote_copy(
                src_ref=source(other),
                dst_ref=target,
                send_sem=send_sems.at[phase],
                recv_sem=recv_sems.at[phase],
                device_id={"kv": other},
                device_id_type=MESH,
            ).start()
            return carry

        lax.fori_loop(1, kv_size, one, 0)

    def send_tp(phase, source, target):
        def one(step, carry):
            pltpu.make_async_remote_copy(
                src_ref=source,
                dst_ref=target,
                send_sem=send_sems.at[phase],
                recv_sem=recv_sems.at[phase],
                device_id={"tp": lax.rem(tp + step, tp_size)},
                device_id_type=MESH,
            ).start()
            return carry

        lax.fori_loop(1, tp_size, one, 0)

    def whole(phase, part):
        return pltpu.make_async_remote_copy(
            src_ref=part,
            dst_ref=part,
            send_sem=send_sems.at[phase],
            recv_sem=recv_sems.at[phase],
            device_id={"tp": tp},
            device_id_type=MESH,
        )

    others = {
        0: r1.at[pl.ds(0, plane - 1)],
        1: r2.at[pl.ds(0, plane - 1)],
        2: r3.at[pl.ds(0, kv_size - 1)],
        3: r4.at[pl.ds(0, kv_size - 1)],
        4: r5.at[pl.ds(0, (plane - 1) * 8)],
        5: r6.at[pl.ds(0, tp_size - 1)],
        6: r7.at[pl.ds(0, plane - 1)],
        7: r8.at[pl.ds(0, plane - 1)],
        8: r9.at[pl.ds(0, tp_size - 1)],
    }

    def arrived(phase):
        whole(phase, others[phase]).wait_recv()

    seqs = tokens.shape[0]
    width = tokens.shape[1]
    pool_lane = pool_row[...]
    diagonal = iota((seqs, seqs), 0) == iota((seqs, seqs), 1)
    spread = jnp.broadcast_to(pool_lane, (seqs, seqs))
    pool_column = jnp.sum(jnp.where(diagonal, spread, 0), axis=1, keepdims=True)
    to_slots = (pool_column == iota((seqs, seqs), 1)).astype(BF16)
    to_seqs = (spread == iota((seqs, seqs), 0)).astype(BF16)
    stream = jnp.dot(to_slots, tokens[...], preferred_element_type=F32)

    wide = iota((seqs, HEAD), 0) == iota((seqs, HEAD), 1)

    def as_lanes(column):
        return jnp.sum(
            jnp.where(wide, jnp.broadcast_to(column, (seqs, HEAD)), 0.0), axis=0, keepdims=True
        )

    def as_column(lanes):
        return jnp.sum(
            jnp.where(wide, jnp.broadcast_to(lanes, (seqs, HEAD)), 0.0), axis=1, keepdims=True
        )

    squares = as_lanes(jnp.sum(stream * stream, axis=1, keepdims=True))
    s1[0] = squares
    r1[me] = squares

    pl.semaphore_wait(barrier, plane - 1 + tp_size - 1)

    send_plane(0, lambda other: s1.at[0], r1.at[me])
    blank = jnp.zeros((seqs, HEAD), F32)
    for part in range(GROUP + 2, 16):
        s2[pl.ds(part, seqs, stride=16), :] = blank
    arrived(0)
    first_sum = as_column(jnp.sum(r1[...], axis=0))
    normed = (stream * lax.rsqrt(first_sum / D + EPSILON) * gains[0:1, :]).astype(BF16)

    loads[0].wait()
    united = jnp.dot(normed, qkv_v[...], preferred_element_type=F32)
    for part in range(GROUP + 2):
        s2[pl.ds(part, seqs, stride=16), :] = united[:, part * HEAD : (part + 1) * HEAD]
    send_plane(1, lambda other: s2.at[pl.ds(pl.multiple_of(other * 16, 16), 16), :], r2.at[me])
    r2[me] = s2[pl.ds(pl.multiple_of(me * 16, 16), 16), :]
    my_seq = pool_smem[me]
    pick = iota((seqs, HEAD), 0) == my_seq
    cosine = jnp.sum(jnp.where(pick, cosines[...], 0.0), axis=0, keepdims=True)
    sine = jnp.sum(jnp.where(pick, sines[...], 0.0), axis=0, keepdims=True)
    rotated = iota((16, HEAD), 0) <= GROUP
    cosine = jnp.where(rotated, jnp.broadcast_to(cosine, (16, HEAD)), 1.0)
    sine = jnp.where(rotated, jnp.broadcast_to(sine, (16, HEAD)), 0.0)
    arrived(1)
    mine = jnp.sum(r2[...], axis=0)
    mine = mine * cosine + pltpu.roll(mine, HEAD // 2, 1) * sine
    mine = mine.astype(BF16)

    s3[...] = mine
    r3[kv] = mine
    send_kv(2, lambda other: s3, r3.at[kv])
    fresh_query = mine[:GROUP].astype(F32)
    fresh_key = mine[GROUP : GROUP + 1].astype(F32)
    fresh_value = mine[GROUP + 1 : GROUP + 2].astype(F32)
    score_scale = HEAD ** (-0.5)
    fresh_score = jnp.sum(fresh_query * fresh_key, axis=1, keepdims=True) * score_scale
    loads[1].wait()
    loads[2].wait()
    arrived(2)
    slots = r3.shape[0]
    rows_now = r3[...].astype(F32)
    new_keys[...] = jnp.concatenate(
        [rows_now[slot, GROUP : GROUP + 1] for slot in range(slots)], axis=0
    ).astype(BF16)
    new_values[...] = jnp.concatenate(
        [rows_now[slot, GROUP + 1 : GROUP + 2] for slot in range(slots)], axis=0
    ).astype(BF16)

    block = keys_v.shape[1]
    position = kv * block + iota((GROUP, block), 1)
    lane = iota((GROUP, HEAD), 1)
    for slot in range(slots):
        limit = len_smem[pool_smem[row * slots + slot]]
        scores = (
            lax.dot_general(
                r3[slot, :GROUP, :],
                keys_v[slot],
                (((1,), (1,)), ((), ())),
                preferred_element_type=F32,
            )
            * score_scale
        )
        allowed = position < limit
        peak = jnp.max(jnp.where(allowed, scores, FLOOR), axis=1, keepdims=True)
        weights = jnp.where(allowed, jnp.exp(scores - peak), 0.0)
        total = jnp.sum(weights, axis=1, keepdims=True)
        product = jnp.dot(weights.astype(BF16), values_v[slot], preferred_element_type=F32)
        s4[slot * 16 : slot * 16 + GROUP, :] = product
        s4[slot * 16 + GROUP : slot * 16 + 16, :] = jnp.where(lane == 0, peak, total)

    send_kv(3, lambda other: s4.at[pl.ds(pl.multiple_of(other * 16, 16), 16), :], r4.at[kv])
    r4[kv] = s4[pl.ds(pl.multiple_of(kv * 16, 16), 16), :]
    arrived(3)
    parts = r4[...]
    peaks = [parts[source, GROUP:, 0:1] for source in range(slots)]
    joint = fresh_score
    for peak in peaks:
        joint = jnp.maximum(joint, peak)
    fresh_weight = jnp.exp(fresh_score - joint)
    total = fresh_weight
    numer = fresh_weight.astype(BF16).astype(F32) * fresh_value
    for source in range(slots):
        fade = jnp.exp(peaks[source] - joint)
        total = total + parts[source, GROUP:, 1:2] * fade
        numer = numer + parts[source, :GROUP] * fade
    mixed = numer / total

    s5[...] = mixed
    r5[pl.ds(pl.multiple_of(me * 8, 8), 8), :] = mixed
    send_plane(4, lambda other: s5, r5.at[pl.ds(pl.multiple_of(me * 8, 8), 8), :])
    loads[3].wait()
    arrived(4)
    mixed_all = jnp.concatenate(
        [r5[pl.ds(head, seqs, stride=8), :].astype(BF16) for head in range(GROUP)], axis=1
    )
    projected = jnp.dot(mixed_all, out_v[...], preferred_element_type=F32)

    s6[...] = projected
    r6[tp] = projected
    send_tp(5, s6, r6.at[tp])
    loads[4].wait()
    loads[5].wait()
    arrived(5)
    projected = r6[0]
    for source in range(1, tp_size):
        projected = projected + r6[source]
    stream_two = (stream + projected).astype(BF16).astype(F32)
    square_column = jnp.broadcast_to(
        jnp.sum(stream_two * stream_two, axis=1, keepdims=True), (seqs, HEAD)
    )
    scaled = (stream_two * gains[1:2, :]).astype(BF16)

    gate = jnp.dot(scaled, gate_v[...], preferred_element_type=F32)
    up = jnp.dot(scaled, up_v[...], preferred_element_type=F32)
    chunks = gate.shape[1] // HEAD
    for part in range(chunks):
        w7[pl.ds(part, seqs, stride=32), :] = gate[:, part * HEAD : (part + 1) * HEAD]
        w7[pl.ds(part + 16, seqs, stride=32), :] = up[:, part * HEAD : (part + 1) * HEAD]
    high = square_column.astype(BF16).astype(F32)
    w7[pl.ds(14, seqs, stride=32), :] = high
    w7[pl.ds(15, seqs, stride=32), :] = square_column - high
    w7[pl.ds(30, seqs, stride=32), :] = blank
    w7[pl.ds(31, seqs, stride=32), :] = blank
    s7[...] = w7[...].astype(BF16)
    send_plane(6, lambda other: s7.at[pl.ds(pl.multiple_of(other * 32, 32), 32), :], r7.at[me])
    r7[me] = s7[pl.ds(pl.multiple_of(me * 32, 32), 32), :]
    loads[6].wait()
    arrived(6)
    sums = jnp.sum(r7[...].astype(F32), axis=0)
    scale = lax.rsqrt((sums[14:15] + sums[15:16]) / D + EPSILON)
    gate = sums[:16] * scale
    up = sums[16:] * scale
    activated = (gate / (1.0 + jnp.exp(-gate)) * up).astype(BF16)

    s8[...] = activated
    r8[me] = activated
    send_plane(7, lambda other: s8, r8.at[me])
    arrived(7)
    w8[...] = r8[...].astype(F32).reshape(w8.shape)
    active_all = jnp.concatenate(
        [w8[pl.ds(part, seqs, stride=16), :].astype(BF16) for part in range(chunks)], axis=1
    )
    down = jnp.dot(active_all, down_v[...], preferred_element_type=F32)

    s9[...] = down
    r9[tp] = down
    send_tp(8, s9, r9.at[tp])
    arrived(8)
    down = r9[0]
    for source in range(1, tp_size):
        down = down + r9[source]
    result = (stream_two + down).astype(BF16)
    layer_out[...] = jnp.dot(to_seqs, result, preferred_element_type=F32).astype(BF16)

    for phase in range(9):
        whole(phase, others[phase]).wait_send()


def local(
    sizes,
    tokens,
    attn_gain,
    w_qkv,
    w_out,
    ffn_gain,
    w_gate,
    w_up,
    w_down,
    cache_keys,
    cache_values,
    cache_len,
    pool_seq,
):
    tp_size, row_size, kv_size = sizes
    seqs, width = tokens.shape
    half = HEAD // 2
    frequency = ROPE_BASE ** (-(jnp.arange(half, dtype=F32) * 2.0 / HEAD))
    angles = cache_len.astype(F32)[:, None] * frequency[None, :]
    cosine = jnp.cos(angles)
    sine = jnp.sin(angles)
    cosines = jnp.concatenate([cosine, cosine], axis=1)
    sines = jnp.concatenate([-sine, sine], axis=1)
    gains = jnp.stack([attn_gain.astype(F32), ffn_gain.astype(F32)])
    plane = row_size * kv_size
    vmem = pl.BlockSpec(memory_space=pltpu.VMEM)
    smem = pl.BlockSpec(memory_space=pltpu.SMEM)
    hbm = pl.BlockSpec(memory_space=pl.ANY)
    scratch = [
        pltpu.VMEM(w_qkv.shape, BF16),
        pltpu.VMEM(w_out.shape, BF16),
        pltpu.VMEM(w_gate.shape, BF16),
        pltpu.VMEM(w_up.shape, BF16),
        pltpu.VMEM(w_down.shape, BF16),
        pltpu.VMEM(cache_keys.shape, BF16),
        pltpu.VMEM(cache_values.shape, BF16),
        pltpu.VMEM((1, 1, HEAD), F32),
        pltpu.VMEM((plane, 1, HEAD), F32),
        pltpu.VMEM((plane * 16, HEAD), F32),
        pltpu.VMEM((plane, 16, HEAD), F32),
        pltpu.VMEM((16, HEAD), BF16),
        pltpu.VMEM((kv_size, 16, HEAD), BF16),
        pltpu.VMEM((kv_size * 16, HEAD), F32),
        pltpu.VMEM((kv_size, 16, HEAD), F32),
        pltpu.VMEM((8, HEAD), F32),
        pltpu.VMEM((plane * 8, HEAD), F32),
        pltpu.VMEM((seqs, width), F32),
        pltpu.VMEM((tp_size, seqs, width), F32),
        pltpu.VMEM((plane * 32, HEAD), F32),
        pltpu.VMEM((plane * 32, HEAD), BF16),
        pltpu.VMEM((plane, 32, HEAD), BF16),
        pltpu.VMEM((16, HEAD), BF16),
        pltpu.VMEM((plane, 16, HEAD), BF16),
        pltpu.VMEM((plane * 16, HEAD), F32),
        pltpu.VMEM((seqs, width), F32),
        pltpu.VMEM((tp_size, seqs, width), F32),
        pltpu.SemaphoreType.DMA((7,)),
        pltpu.SemaphoreType.DMA((9,)),
        pltpu.SemaphoreType.DMA((9,)),
    ]
    return pl.pallas_call(
        functools.partial(kernel, tp_size, row_size, kv_size),
        out_shape=(
            jax.ShapeDtypeStruct((seqs, width), BF16),
            jax.ShapeDtypeStruct((kv_size, HEAD), BF16),
            jax.ShapeDtypeStruct((kv_size, HEAD), BF16),
        ),
        in_specs=[smem, smem] + [vmem] * 5 + [hbm] * 7,
        out_specs=(vmem, vmem, vmem),
        scratch_shapes=scratch,
        compiler_params=pltpu.CompilerParams(
            collective_id=0, has_side_effects=True, vmem_limit_bytes=40 * 1024 * 1024
        ),
    )(
        pool_seq,
        cache_len,
        pool_seq.reshape(1, -1),
        tokens,
        gains,
        cosines,
        sines,
        w_qkv,
        w_out,
        w_gate,
        w_up,
        w_down,
        cache_keys,
        cache_values,
    )


def solution(mesh):
    sizes = (mesh.shape["tp"], mesh.shape["row"], mesh.shape["kv"])
    return jax.shard_map(
        functools.partial(local, sizes),
        mesh=mesh,
        in_specs=(
            P(None, ("row", "kv")),
            P(("row", "kv")),
            P(("row", "kv"), "tp"),
            P("tp", ("row", "kv")),
            P(("row", "kv")),
            P(("row", "kv"), "tp"),
            P(("row", "kv"), "tp"),
            P("tp", ("row", "kv")),
            P("row", "kv", "tp"),
            P("row", "kv", "tp"),
            P(),
            P(),
        ),
        out_specs=(P(None, ("row", "kv")), P("row", "tp"), P("row", "tp")),
        check_vma=False,
    )
```

time: 501 us -> 91.1 us (0.18)
  blocking collectives: 286 us -> 0 us
  waiting for transfers between devices: 175 us -> 0 us
  Pallas kernels: 0 us -> 73.9 us
  between operations: 14.3 us -> 0.67 us
  matrix products: 10.6 us -> 0 us
  local copies, waits for them, and re-layouts: 5.39 us -> 15.1 us
  other arithmetic: 8.26 us -> 0.9 us
    psum x5 -> x0, blocking collectives: 222 us -> none  [the longest x1 64.3 us: local(): first_sum = lax.psum(jnp.sum(stream * stream, axis=1), ('row', 'kv'))]
    psum x1 -> x0, waiting for transfers between devices: 151 us -> none  [local(): lax.psum((jnp.dot(normed_two, w_gate, preferred_element_type=jnp.float32)...]
    pallas_call x0 -> x1, Pallas kernels: none -> 73.9 us  [local(): pl.pallas_call(functools.partial(kernel, tp_size, row_size, kv_size), out...]
    all_gather x4 -> x0, blocking collectives: 64.2 us -> none  [the longest x3 55.2 us: combined_all(): pieces = jax.tree.map(lambda part: lax.all_gather(part, axis), value)]
    reduce_scatter x1 -> x0, waiting for transfers between devices: 24.6 us -> none  [local(): lax.psum_scatter(jnp.dot(ordered, w_qkv, preferred_element_type=jnp.float...]
    unnamed x11 -> x23, local copies, waits for them, and re-layouts: 0.03 us -> 13.8 us
    dot_general x8 -> x0, matrix products: 10.6 us -> none  [the longest x1 3.76 us: one_span(): jnp.einsum('sgqd,stgd->sgqt', queries, keys_part, preferred_element_type=...]
  transfers between devices with their start and end apart: 2 -> 0, of which waited for: 2 -> 0; matrix products, arithmetic and copies ran while one was open for 1% -> 0% of each run, Pallas kernels for 0% -> 0%
where the time goes in v1:
time: 91.1 us; the launch traced here: 90.6 us
  Pallas kernels  73.9 us (81%)
  local copies, waits for them, and re-layouts  15.1 us (17%)
    pallas_call x1, Pallas kernels, local(): pl.pallas_call(functools.partial(kernel, tp_size, row_size, kv_size), out...  73.9 us
    unnamed x23, local copies, waits for them, and re-layouts  13.8 us

profile of v1, /device:TPU:1, one launch (start us, length us, event | category | flops | bytes accessed | tf_op | source)
XLA Modules:
  0.0 90.6 jit_solution(647564836096310163)
XLA Ops:
  0.6 0.7 convert_element_type.2
  1.3 0.1 fusion
  1.5 0.1 pad_maximum_fusion
  1.5 0.7 stack.13
  2.2 0.7 stack.14
  2.9 0.0 copy-start
  2.9 2.2 %copy-done = bf16[8,2048,128]{2,1,0:T(8,128)(2,1)S(1)} copy-done((bf16[8,2048,128]{2,1,0:T(8,128)(2,1)S(1)}, bf16[8,2048,128]{2,1,0:T(8,128)(2,1)}, u32[]{:S(2)}) %copy-start) | copy-done | bytes 4194328
  5.1 0.0 copy-start.1
  5.1 2.2 %copy-done.1 = bf16[8,2048,128]{2,1,0:T(8,128)(2,1)S(1)} copy-done((bf16[8,2048,128]{2,1,0:T(8,128)(2,1)S(1)}, bf16[8,2048,128]{2,1,0:T(8,128)(2,1)}, u32[]{:S(2)}) %copy-start.1) | copy-done | bytes 4194328
  7.2 0.0 copy-start.2
  7.2 1.2 %copy-done.2 = bf16[256,1792]{1,0:T(8,128)(2,1)S(1)} copy-done((bf16[256,1792]{1,0:T(8,128)(2,1)S(1)}, bf16[256,1792]{1,0:T(8,128)(2,1)}, u32[]{:S(2)}) %copy-start.2) | copy-done | bytes 917528
  8.4 0.0 copy-start.3
  8.4 1.2 %copy-done.3 = bf16[256,1792]{1,0:T(8,128)(2,1)S(1)} copy-done((bf16[256,1792]{1,0:T(8,128)(2,1)S(1)}, bf16[256,1792]{1,0:T(8,128)(2,1)}, u32[]{:S(2)}) %copy-start.3) | copy-done | bytes 917528
  9.6 0.0 copy-start.4
  9.6 1.2 %copy-done.4 = bf16[1792,256]{1,0:T(8,128)(2,1)S(1)} copy-done((bf16[1792,256]{1,0:T(8,128)(2,1)S(1)}, bf16[1792,256]{1,0:T(8,128)(2,1)}, u32[]{:S(2)}) %copy-start.4) | copy-done | bytes 917528
  10.8 0.0 copy-start.5
  10.8 1.1 %copy-done.5 = bf16[256,1280]{1,0:T(8,128)(2,1)S(1)} copy-done((bf16[256,1280]{1,0:T(8,128)(2,1)S(1)}, bf16[256,1280]{1,0:T(8,128)(2,1)}, u32[]{:S(2)}) %copy-start.5) | copy-done | bytes 655384
  11.9 0.0 copy-start.6
  11.9 1.0 %copy-done.6 = bf16[1024,256]{1,0:T(8,128)(2,1)S(1)} copy-done((bf16[1024,256]{1,0:T(8,128)(2,1)S(1)}, bf16[1024,256]{1,0:T(8,128)(2,1)}, u32[]{:S(2)}) %copy-start.6) | copy-done | bytes 524312
  12.9 0.0 copy-start.7
  12.9 0.7 copy-done.7
  13.6 0.0 copy-start.8
  13.6 0.7 copy-done.8
  14.3 0.0 copy-start.9
  14.3 0.7 copy-done.9
  14.9 73.9 %shard_map.139 = (bf16[32,256]{1,0:T(8,128)(2,1)S(1)}, bf16[8,128]{1,0:T(8,128)(2,1)S(1)}, bf16[8,128]{1,0:T(8,128)(2,1)S(1)}) custom-call(s32[32]{0:T(128)S(1)} %copy-done.8, s32[32]{0:T(128)S(1)} %copy-done.9, s32[1,32]{1,0:T(1,128)S(1)} %bitcast.1, bf16[32,256]{1,0:T(8,128)(2,1)S(1)} %copy-done.7, f32[2,256]{1,0:T(2,128)S(1)} %maximum_convert_fusion.gains, ...), custom_call_target="tpu_custom_call" | custom-call | tf_op jit(solution)/shard_map/pallas_call | solution.py:434
  88.9 0.6 copy.18
  89.5 0.6 copy.19
  90.0 0.6 copy.20
  (2 shorter events, 0.0 us)
Async XLA Ops:
  2.9 2.2 %copy-start = (bf16[8,2048,128]{2,1,0:T(8,128)(2,1)S(1)}, bf16[8,2048,128]{2,1,0:T(8,128)(2,1)}, u32[]{:S(2)}) copy-start(bf16[8,2048,128]{2,1,0:T(8,128)(2,1)} %cache_keys.1) | copy-start | bytes 12582916
  5.1 2.2 %copy-start.1 = (bf16[8,2048,128]{2,1,0:T(8,128)(2,1)S(1)}, bf16[8,2048,128]{2,1,0:T(8,128)(2,1)}, u32[]{:S(2)}) copy-start(bf16[8,2048,128]{2,1,0:T(8,128)(2,1)} %cache_values.1) | copy-start | bytes 12582916
  7.2 1.2 %copy-start.2 = (bf16[256,1792]{1,0:T(8,128)(2,1)S(1)}, bf16[256,1792]{1,0:T(8,128)(2,1)}, u32[]{:S(2)}) copy-start(bf16[256,1792]{1,0:T(8,128)(2,1)} %w_gate.1) | copy-start | bytes 2752516
  8.4 1.2 %copy-start.3 = (bf16[256,1792]{1,0:T(8,128)(2,1)S(1)}, bf16[256,1792]{1,0:T(8,128)(2,1)}, u32[]{:S(2)}) copy-start(bf16[256,1792]{1,0:T(8,128)(2,1)} %w_up.1) | copy-start | bytes 2752516
  9.6 1.2 %copy-start.4 = (bf16[1792,256]{1,0:T(8,128)(2,1)S(1)}, bf16[1792,256]{1,0:T(8,128)(2,1)}, u32[]{:S(2)}) copy-start(bf16[1792,256]{1,0:T(8,128)(2,1)} %w_down.1) | copy-start | bytes 2752516
  10.8 1.1 %copy-start.5 = (bf16[256,1280]{1,0:T(8,128)(2,1)S(1)}, bf16[256,1280]{1,0:T(8,128)(2,1)}, u32[]{:S(2)}) copy-start(bf16[256,1280]{1,0:T(8,128)(2,1)} %w_qkv.1) | copy-start | bytes 1966084
  11.9 1.0 %copy-start.6 = (bf16[1024,256]{1,0:T(8,128)(2,1)S(1)}, bf16[1024,256]{1,0:T(8,128)(2,1)}, u32[]{:S(2)}) copy-start(bf16[1024,256]{1,0:T(8,128)(2,1)} %w_out.1) | copy-start | bytes 1572868
  12.9 0.7 copy-start.7
  13.6 0.7 copy-start.8
  14.3 0.7 copy-start.9

commit v2 on v1

v2 whole, which is shorter than its diff:
```python
import functools

import jax
import jax.numpy as jnp
from jax import lax
from jax.experimental import pallas as pl
from jax.experimental.pallas import tpu as pltpu
from jax.sharding import PartitionSpec as P

D = 8192
HEAD = 128
GROUP = 8
EPSILON = 1e-05
ROPE_BASE = 500000.0
FLOOR = -1e30
MESH = pl.DeviceIdType.MESH
F32 = jnp.float32
BF16 = jnp.bfloat16


def iota(shape, dim):
    return lax.broadcasted_iota(jnp.int32, shape, dim)


def far_first(index, size):
    half = (index + 1) // 2
    return size // 2 + (1 - 2 * lax.rem(index, 2)) * half


def kernel(
    tp_size,
    row_size,
    kv_size,
    frequency_hbm,
    pool_hbm,
    len_hbm,
    tokens_hbm,
    attn_hbm,
    ffn_hbm,
    w_qkv,
    w_out,
    w_gate,
    w_up,
    w_down,
    cache_keys,
    cache_values,
    layer_out,
    new_keys,
    new_values,
    frequency,
    pool_smem,
    len_smem,
    tokens,
    attn_gain,
    ffn_gain,
    qkv_v,
    out_v,
    gate_v,
    up_v,
    down_v,
    keys_v,
    values_v,
    s1,
    r1,
    s2,
    r2,
    sf,
    rf,
    s3,
    r3,
    sp,
    rp,
    s4,
    r4,
    s5,
    r5,
    s6,
    r6,
    w7,
    s7,
    r7,
    s8,
    r8,
    w8,
    s9,
    r9,
    s_out,
    load_sems,
    send_sems,
    recv_sems,
    query_sems,
    out_sems,
):
    plane = row_size * kv_size
    tp = lax.axis_index("tp")
    row = lax.axis_index("row")
    kv = lax.axis_index("kv")
    me = row * kv_size + kv

    barrier = pltpu.get_barrier_semaphore()

    def plane_partner(index):
        other_row = lax.rem(row + far_first(lax.rem(index, row_size), row_size), row_size)
        other_kv = lax.rem(kv + far_first(index // row_size, kv_size), kv_size)
        return other_row, other_kv

    def greet_plane(index, carry):
        other_row, other_kv = plane_partner(index)
        pl.semaphore_signal(
            barrier,
            inc=1,
            device_id={"row": other_row, "kv": other_kv},
            device_id_type=MESH,
        )
        return carry

    def greet_tp(step, carry):
        pl.semaphore_signal(
            barrier, inc=1, device_id={"tp": lax.rem(tp + step, tp_size)}, device_id_type=MESH
        )
        return carry

    lax.fori_loop(0, plane - 1, greet_plane, 0)
    lax.fori_loop(1, tp_size, greet_tp, 0)

    pending = {}
    for index, (name, source, target) in enumerate(
        (
            ("pool", pool_hbm, pool_smem),
            ("tokens", tokens_hbm, tokens),
            ("len", len_hbm, len_smem),
            ("attn", attn_hbm, attn_gain),
            ("frequency", frequency_hbm, frequency),
            ("qkv", w_qkv, qkv_v),
            ("keys", cache_keys, keys_v),
            ("values", cache_values, values_v),
            ("out", w_out, out_v),
            ("ffn", ffn_hbm, ffn_gain),
            ("gate", w_gate, gate_v),
            ("up", w_up, up_v),
            ("down", w_down, down_v),
        )
    ):
        pending[name] = pltpu.make_async_copy(source, target, load_sems.at[index])
        pending[name].start()

    def need(*names):
        for name in names:
            pending.pop(name).wait()

    sent = []

    def send_plane(phase, source, target):
        sent.append(phase)

        def one(index, carry):
            other_row, other_kv = plane_partner(index)
            pltpu.make_async_remote_copy(
                src_ref=source(other_row * kv_size + other_kv),
                dst_ref=target,
                send_sem=send_sems.at[phase],
                recv_sem=recv_sems.at[phase],
                device_id={"row": other_row, "kv": other_kv},
                device_id_type=MESH,
            ).start()
            return carry

        lax.fori_loop(0, plane - 1, one, 0)

    def send_tp(phase, source, target):
        sent.append(phase)

        def one(index, carry):
            pltpu.make_async_remote_copy(
                src_ref=source,
                dst_ref=target,
                send_sem=send_sems.at[phase],
                recv_sem=recv_sems.at[phase],
                device_id={"tp": lax.rem(tp + far_first(index, tp_size), tp_size)},
                device_id_type=MESH,
            ).start()
            return carry

        lax.fori_loop(0, tp_size - 1, one, 0)

    def whole(phase, part):
        return pltpu.make_async_remote_copy(
            src_ref=part,
            dst_ref=part,
            send_sem=send_sems.at[phase],
            recv_sem=recv_sems.at[phase],
            device_id={"tp": tp},
            device_id_type=MESH,
        )

    others = {
        0: r1.at[pl.ds(0, plane - 1)],
        1: r2.at[pl.ds(0, plane - 1)],
        2: r3.at[pl.ds(0, kv_size - 1)],
        3: r4.at[pl.ds(0, kv_size - 1)],
        4: r5.at[pl.ds(0, (plane - 1) * 8)],
        5: r6.at[pl.ds(0, tp_size - 1)],
        6: r7.at[pl.ds(0, plane - 1)],
        7: r8.at[pl.ds(0, plane - 1)],
        8: r9.at[pl.ds(0, tp_size - 1)],
    }

    def drain():
        for phase in sent:
            whole(phase, others[phase]).wait_send()

        if 1 in sent:
            @pl.when(owns_fresh)
            def _():
                whole(9, rf.at[pl.ds(0, 2 * row_size - 1)]).wait_send()

            @pl.when(jnp.logical_not(owns_fresh))
            def _():
                whole(9, rf.at[pl.ds(0, 2 * row_size)]).wait_send()

        if 2 in sent:
            @pl.when(owns_fresh)
            def _():
                whole(10, r3.at[pl.ds(0, kv_size - 1)]).wait_send()

    def arrived(phase):
        whole(phase, others[phase]).wait_recv()

    seqs = tokens.shape[0]
    width = tokens.shape[1]
    need("pool", "tokens")
    holder = jnp.zeros((seqs, seqs), jnp.int32)
    held = jnp.zeros((seqs, seqs), jnp.int32)
    for slot in range(seqs):
        seq = pool_smem[slot]
        holder = jnp.where(iota((seqs, seqs), 0) == slot, seq, holder)
        held = jnp.where(iota((seqs, seqs), 1) == slot, seq, held)
    to_slots = (holder == iota((seqs, seqs), 1)).astype(BF16)
    to_seqs = (held == iota((seqs, seqs), 0)).astype(BF16)
    stream = jnp.dot(to_slots, tokens[...], preferred_element_type=F32)

    wide = iota((seqs, HEAD), 0) == iota((seqs, HEAD), 1)

    def as_lanes(column):
        return jnp.sum(
            jnp.where(wide, jnp.broadcast_to(column, (seqs, HEAD)), 0.0), axis=0, keepdims=True
        )

    def as_column(lanes):
        return jnp.sum(
            jnp.where(wide, jnp.broadcast_to(lanes, (seqs, HEAD)), 0.0), axis=1, keepdims=True
        )

    squares = as_lanes(jnp.sum(stream * stream, axis=1, keepdims=True))
    s1[0] = squares
    r1[me] = squares

    pl.semaphore_wait(barrier, plane - 1 + tp_size - 1)

    send_plane(0, lambda other: s1.at[0], r1.at[me])
    arrived(0)
    first_sum = as_column(jnp.sum(r1[...], axis=0))
    need("attn", "len", "frequency", "qkv")
    gain = attn_gain[...].astype(F32).reshape(1, width)
    normed = (stream * lax.rsqrt(first_sum / D + EPSILON) * gain).astype(BF16)

    united = jnp.dot(normed, qkv_v[...], preferred_element_type=F32)
    for part in range(GROUP):
        s2[pl.ds(part, seqs, stride=GROUP), :] = united[:, part * HEAD : (part + 1) * HEAD]
    for part in range(2):
        sf[part] = united[:, (GROUP + part) * HEAD : (GROUP + part + 1) * HEAD]
    send_plane(1, lambda other: s2.at[pl.ds(pl.multiple_of(other * 8, 8), 8), :], r2.at[me])
    r2[me] = s2[pl.ds(pl.multiple_of(me * 8, 8), 8), :]

    def send_fresh(index, carry):
        owner_row, part = index // 2, lax.rem(index, 2)
        owner_kv = index

        @pl.when(jnp.logical_not((owner_row == row) & (owner_kv == kv)))
        def _():
            pltpu.make_async_remote_copy(
                src_ref=sf.at[part, pl.ds(pl.multiple_of(owner_row * kv_size, 8), kv_size), :],
                dst_ref=rf.at[me],
                send_sem=send_sems.at[9],
                recv_sem=recv_sems.at[9],
                device_id={"row": owner_row, "kv": owner_kv},
                device_id_type=MESH,
            ).start()

        return carry

    lax.fori_loop(0, 2 * row_size, send_fresh, 0)
    owns_fresh = kv // 2 == row
    fresh_part = lax.rem(kv, 2)
    lane_sign = jnp.where(iota((1, HEAD), 1) < HEAD // 2, -1.0, 1.0)
    angle = len_smem[pool_smem[me]].astype(F32) * frequency[...]
    cosine = jnp.cos(angle)
    sine = jnp.sin(angle) * lane_sign
    slots = kv_size
    limits = [len_smem[pool_smem[row * slots + slot]] for slot in range(slots)]
    arrived(1)
    mine = jnp.sum(r2[...], axis=0)
    mine = mine * cosine + pltpu.roll(mine, HEAD // 2, 1) * sine
    mine = jnp.concatenate([mine, jnp.zeros_like(mine)], axis=0).astype(BF16)

    s3[...] = mine
    r3[kv] = mine

    def query_copy(offset, target, index):
        return pltpu.make_async_remote_copy(
            src_ref=s3,
            dst_ref=r3.at[target],
            send_sem=send_sems.at[2],
            recv_sem=query_sems.at[index],
            device_id={"kv": lax.rem(kv + offset, kv_size)},
            device_id_type=MESH,
        )

    for index in range(kv_size - 1):
        offset = (4, 3, 5, 2, 6, 1, 7)[index]
        query_copy(offset, kv, kv_size - offset).start()
    sent.append(2)

    @pl.when(owns_fresh)
    def _():
        rf[me] = sf[fresh_part, pl.ds(pl.multiple_of(row * kv_size, 8), kv_size), :]
        column = jnp.zeros((slots, HEAD), jnp.int32)
        for slot in range(slots):
            column = jnp.where(iota((slots, HEAD), 0) == slot, limits[slot], column)
        angles = column.astype(F32) * frequency[...]
        cosines = jnp.where(fresh_part == 0, jnp.cos(angles), 1.0)
        sines = jnp.where(fresh_part == 0, jnp.sin(angles) * lane_sign, 0.0)
        whole(9, rf.at[pl.ds(0, plane - 1)]).wait_recv()
        fresh = jnp.sum(rf[...], axis=0)
        fresh = fresh * cosines + pltpu.roll(fresh, HEAD // 2, 1) * sines
        fresh = jnp.concatenate([fresh, jnp.zeros_like(fresh)], axis=0).astype(BF16)
        sp[...] = fresh
        rp[fresh_part] = fresh

        def share(step, carry):
            pltpu.make_async_remote_copy(
                src_ref=sp,
                dst_ref=rp.at[fresh_part],
                send_sem=send_sems.at[10],
                recv_sem=recv_sems.at[10],
                device_id={"kv": lax.rem(kv + step, kv_size)},
                device_id_type=MESH,
            ).start()
            return carry

        lax.fori_loop(1, kv_size, share, 0)

    need("keys", "values")
    block = keys_v.shape[1]
    score_scale = HEAD ** (-0.5)
    position = kv * block + iota((GROUP, block), 1)
    lane = iota((GROUP, HEAD), 1)
    for group in ((0,), (1, 7), (2, 6), (4,), (3, 5)):
        at = [lax.rem(kv + offset, kv_size) for offset in group]
        for offset, slot in zip(group, at):
            if offset:
                query_copy(offset, slot, offset).wait_recv()
        scores = [
            lax.dot_general(
                r3[slot, :GROUP, :],
                keys_v[slot],
                (((1,), (1,)), ((), ())),
                preferred_element_type=F32,
            )
            * score_scale
            for slot in at
        ]
        results = []
        for slot, score in zip(at, scores):
            limit = len_smem[pool_smem[row * slots + slot]]
            allowed = position < limit
            peak = jnp.max(jnp.where(allowed, score, FLOOR), axis=1, keepdims=True)
            weights = jnp.where(allowed, jnp.exp(score - peak), 0.0)
            total = jnp.sum(weights, axis=1, keepdims=True)
            product = jnp.dot(weights.astype(BF16), values_v[slot], preferred_element_type=F32)
            results.append((product, jnp.where(lane == 0, peak, total)))
        for offset, slot, (product, stats) in zip(group, at, results):
            if offset == 0:
                r4[kv, :GROUP] = product
                r4[kv, GROUP:] = stats
            else:
                s4[slot, :GROUP] = product
                s4[slot, GROUP:] = stats
                pltpu.make_async_remote_copy(
                    src_ref=s4.at[slot],
                    dst_ref=r4.at[kv],
                    send_sem=send_sems.at[3],
                    recv_sem=recv_sems.at[3],
                    device_id={"kv": slot},
                    device_id_type=MESH,
                ).start()
    sent.append(3)

    @pl.when(owns_fresh)
    def _():
        whole(10, rp.at[0]).wait_recv()

    @pl.when(jnp.logical_not(owns_fresh))
    def _():
        whole(10, rp).wait_recv()

    keys_out = pltpu.make_async_copy(rp.at[0], new_keys, out_sems.at[0])
    values_out = pltpu.make_async_copy(rp.at[1], new_values, out_sems.at[1])
    keys_out.start()
    values_out.start()
    this_slot = iota((slots, HEAD), 0) == kv
    fresh_key = jnp.sum(
        jnp.where(this_slot, rp[0].astype(F32)[:slots], 0.0), axis=0, keepdims=True
    )
    fresh_value = jnp.sum(
        jnp.where(this_slot, rp[1].astype(F32)[:slots], 0.0), axis=0, keepdims=True
    )
    fresh_query = mine.astype(F32)[:GROUP]
    fresh_score = jnp.sum(fresh_query * fresh_key, axis=1, keepdims=True) * score_scale
    arrived(3)
    parts = r4[...]
    peaks = [parts[source, GROUP:, 0:1] for source in range(slots)]
    joint = fresh_score
    for peak in peaks:
        joint = jnp.maximum(joint, peak)
    fresh_weight = jnp.exp(fresh_score - joint)
    total = fresh_weight
    numer = fresh_weight.astype(BF16).astype(F32) * fresh_value
    for source in range(slots):
        fade = jnp.exp(peaks[source] - joint)
        total = total + parts[source, GROUP:, 1:2] * fade
        numer = numer + parts[source, :GROUP] * fade
    mixed = numer / total

    s5[...] = mixed
    r5[pl.ds(pl.multiple_of(me * 8, 8), 8), :] = mixed
    send_plane(4, lambda other: s5, r5.at[pl.ds(pl.multiple_of(me * 8, 8), 8), :])
    need("out")
    arrived(4)
    mixed_all = jnp.concatenate(
        [r5[pl.ds(head, seqs, stride=8), :].astype(BF16) for head in range(GROUP)], axis=1
    )
    projected = jnp.dot(mixed_all, out_v[...], preferred_element_type=F32)

    projected = projected.astype(BF16)
    s6[...] = projected
    r6[tp] = projected
    send_tp(5, s6, r6.at[tp])
    need("ffn", "gate", "up")
    arrived(5)
    projected = r6[0].astype(F32)
    for source in range(1, tp_size):
        projected = projected + r6[source].astype(F32)
    stream_two = (stream + projected).astype(BF16).astype(F32)
    square_column = jnp.broadcast_to(
        jnp.sum(stream_two * stream_two, axis=1, keepdims=True), (seqs, HEAD)
    )
    scaled = (stream_two * ffn_gain[...].astype(F32).reshape(1, width)).astype(BF16)

    gate = jnp.dot(scaled, gate_v[...], preferred_element_type=F32)
    up = jnp.dot(scaled, up_v[...], preferred_element_type=F32)
    chunks = gate.shape[1] // HEAD
    for part in range(chunks):
        w7[pl.ds(part, seqs, stride=32), :] = gate[:, part * HEAD : (part + 1) * HEAD]
        w7[pl.ds(part + 16, seqs, stride=32), :] = up[:, part * HEAD : (part + 1) * HEAD]
    blank = jnp.zeros((seqs, HEAD), F32)
    high = square_column.astype(BF16).astype(F32)
    w7[pl.ds(14, seqs, stride=32), :] = high
    w7[pl.ds(15, seqs, stride=32), :] = square_column - high
    w7[pl.ds(30, seqs, stride=32), :] = blank
    w7[pl.ds(31, seqs, stride=32), :] = blank
    s7[...] = w7[...].astype(BF16)
    send_plane(6, lambda other: s7.at[pl.ds(pl.multiple_of(other * 32, 32), 32), :], r7.at[me])
    r7[me] = s7[pl.ds(pl.multiple_of(me * 32, 32), 32), :]
    need("down")
    arrived(6)
    sums = jnp.sum(r7[...].astype(F32), axis=0)
    scale = lax.rsqrt((sums[14:15] + sums[15:16]) / D + EPSILON)
    gate = sums[:16] * scale
    up = sums[16:] * scale
    activated = (gate / (1.0 + jnp.exp(-gate)) * up).astype(BF16)

    s8[...] = activated
    r8[me] = activated
    send_plane(7, lambda other: s8, r8.at[me])
    arrived(7)
    w8[...] = r8[...].astype(F32).reshape(w8.shape)
    active_all = jnp.concatenate(
        [w8[pl.ds(part, seqs, stride=16), :].astype(BF16) for part in range(chunks)], axis=1
    )
    down = jnp.dot(active_all, down_v[...], preferred_element_type=F32)

    down = down.astype(BF16)
    s9[...] = down
    r9[tp] = down
    send_tp(8, s9, r9.at[tp])
    arrived(8)
    down = r9[0].astype(F32)
    for source in range(1, tp_size):
        down = down + r9[source].astype(F32)
    result = (stream_two + down).astype(BF16)
    s_out[...] = jnp.dot(to_seqs, result, preferred_element_type=F32).astype(BF16)
    layer_copy = pltpu.make_async_copy(s_out, layer_out, out_sems.at[2])
    layer_copy.start()
    keys_out.wait()
    values_out.wait()
    layer_copy.wait()
    drain()


def local(
    sizes,
    tokens,
    attn_gain,
    w_qkv,
    w_out,
    ffn_gain,
    w_gate,
    w_up,
    w_down,
    cache_keys,
    cache_values,
    cache_len,
    pool_seq,
):
    tp_size, row_size, kv_size = sizes
    seqs, width = tokens.shape
    half = HEAD // 2
    pair = lax.rem(jnp.arange(HEAD, dtype=jnp.int32), half).astype(F32)
    frequency = (ROPE_BASE ** (-(pair * 2.0 / HEAD))).reshape(1, HEAD)
    plane = row_size * kv_size
    hbm = pl.BlockSpec(memory_space=pltpu.HBM)
    scratch = [
        pltpu.VMEM((1, HEAD), F32),
        pltpu.SMEM(pool_seq.shape, jnp.int32),
        pltpu.SMEM(cache_len.shape, jnp.int32),
        pltpu.VMEM(tokens.shape, BF16),
        pltpu.VMEM(attn_gain.shape, BF16),
        pltpu.VMEM(ffn_gain.shape, BF16),
        pltpu.VMEM(w_qkv.shape, BF16),
        pltpu.VMEM(w_out.shape, BF16),
        pltpu.VMEM(w_gate.shape, BF16),
        pltpu.VMEM(w_up.shape, BF16),
        pltpu.VMEM(w_down.shape, BF16),
        pltpu.VMEM(cache_keys.shape, BF16),
        pltpu.VMEM(cache_values.shape, BF16),
        pltpu.VMEM((1, 1, HEAD), F32),
        pltpu.VMEM((plane, 1, HEAD), F32),
        pltpu.VMEM((plane * 8, HEAD), F32),
        pltpu.VMEM((plane, 8, HEAD), F32),
        pltpu.VMEM((2, plane, HEAD), F32),
        pltpu.VMEM((plane, 8, HEAD), F32),
        pltpu.VMEM((16, HEAD), BF16),
        pltpu.VMEM((kv_size, 16, HEAD), BF16),
        pltpu.VMEM((16, HEAD), BF16),
        pltpu.VMEM((2, 16, HEAD), BF16),
        pltpu.VMEM((kv_size, 16, HEAD), F32),
        pltpu.VMEM((kv_size, 16, HEAD), F32),
        pltpu.VMEM((8, HEAD), F32),
        pltpu.VMEM((plane * 8, HEAD), F32),
        pltpu.VMEM((seqs, width), BF16),
        pltpu.VMEM((tp_size, seqs, width), BF16),
        pltpu.VMEM((plane * 32, HEAD), F32),
        pltpu.VMEM((plane * 32, HEAD), BF16),
        pltpu.VMEM((plane, 32, HEAD), BF16),
        pltpu.VMEM((16, HEAD), BF16),
        pltpu.VMEM((plane, 16, HEAD), BF16),
        pltpu.VMEM((plane * 16, HEAD), F32),
        pltpu.VMEM((seqs, width), BF16),
        pltpu.VMEM((tp_size, seqs, width), BF16),
        pltpu.VMEM((seqs, width), BF16),
        pltpu.SemaphoreType.DMA((13,)),
        pltpu.SemaphoreType.DMA((11,)),
        pltpu.SemaphoreType.DMA((11,)),
        pltpu.SemaphoreType.DMA((kv_size,)),
        pltpu.SemaphoreType.DMA((3,)),
    ]
    result, keys, values = pl.pallas_call(
        functools.partial(kernel, tp_size, row_size, kv_size),
        out_shape=(
            jax.ShapeDtypeStruct((seqs, width), BF16),
            jax.ShapeDtypeStruct((16, HEAD), BF16),
            jax.ShapeDtypeStruct((16, HEAD), BF16),
        ),
        in_specs=[hbm] * 13,
        out_specs=(hbm, hbm, hbm),
        scratch_shapes=scratch,
        compiler_params=pltpu.CompilerParams(
            collective_id=0, has_side_effects=True, vmem_limit_bytes=56 * 1024 * 1024
        ),
    )(
        frequency,
        pool_seq,
        cache_len,
        tokens,
        attn_gain,
        ffn_gain,
        w_qkv,
        w_out,
        w_gate,
        w_up,
        w_down,
        cache_keys,
        cache_values,
    )
    return result, keys[:kv_size], values[:kv_size]


def solution(mesh):
    sizes = (mesh.shape["tp"], mesh.shape["row"], mesh.shape["kv"])
    return jax.shard_map(
        functools.partial(local, sizes),
        mesh=mesh,
        in_specs=(
            P(None, ("row", "kv")),
            P(("row", "kv")),
            P(("row", "kv"), "tp"),
            P("tp", ("row", "kv")),
            P(("row", "kv")),
            P(("row", "kv"), "tp"),
            P(("row", "kv"), "tp"),
            P("tp", ("row", "kv")),
            P("row", "kv", "tp"),
            P("row", "kv", "tp"),
            P(),
            P(),
        ),
        out_specs=(P(None, ("row", "kv")), P("row", "tp"), P("row", "tp")),
        check_vma=False,
    )
```

time: 91.1 us -> 70.8 us (0.78)
  local copies, waits for them, and re-layouts: 15.1 us -> 3.8 us
  Pallas kernels: 73.9 us -> 65.6 us
    unnamed x23 -> x1, local copies, waits for them, and re-layouts: 13.8 us -> 1.32 us
    pallas_call x1, Pallas kernels: 73.9 us -> 65.6 us  [local(): pl.pallas_call(functools.partial(kernel, tp_size, row_size, kv_size), out...]
    slice x0 -> x2, local copies, waits for them, and re-layouts: none -> 2.48 us  [local(): return (result, keys[:kv_size], values[:kv_size])]
    another operation x2 -> x0, local copies, waits for them, and re-layouts: 1.32 us -> none  [local(): gains = jnp.stack([attn_gain.astype(F32), ffn_gain.astype(F32)])]
where the time goes in v2:
time: 70.8 us; the launch traced here: 70.5 us
  Pallas kernels  65.6 us (93%)
  local copies, waits for them, and re-layouts  3.8 us (5%)
    pallas_call x1, Pallas kernels, local(): pl.pallas_call(functools.partial(kernel, tp_size, row_size, kv_size), out...  65.6 us
    slice x2, local copies, waits for them, and re-layouts, local(): return (result, keys[:kv_size], values[:kv_size])  2.48 us

profile of v2, /device:TPU:1, one launch (start us, length us, event | category | flops | bytes accessed | tf_op | source)
XLA Modules:
  0.0 70.5 jit_solution(1820883736776919332)
XLA Ops:
  0.6 0.5 negate_power_fusion.frequency_hbm
  1.2 65.6 %shard_map.139 = (bf16[32,256]{1,0:T(8,128)(2,1)}, bf16[16,128]{1,0:T(8,128)(2,1)}, bf16[16,128]{1,0:T(8,128)(2,1)}) custom-call(f32[1,128]{1,0:T(1,128)} %negate_power_fusion.frequency_hbm, s32[32]{0:T(128)} %pool_hbm.1, s32[32]{0:T(128)} %len_hbm.1, bf16[32,256]{1,0:T(8,128)(2,1)} %tokens_hbm.1, bf16[256]{0:T(256)(128)(2,1)} %attn_hbm.1, ...), custom_call_target="tpu_custom_call" | custom-call | tf_op jit(solution)/shard_map/pallas_call | solution.py:578
  66.7 1.2 %slice.6 = bf16[8,128]{1,0:T(8,128)(2,1)} slice(bf16[16,128]{1,0:T(8,128)(2,1)} %get-tuple-element.7), slice={[0:8], [0:128]} | slice | bytes 4096 | tf_op jit(solution)/shard_map/slice | solution.py:606
  68.0 1.2 %slice.7 = bf16[8,128]{1,0:T(8,128)(2,1)} slice(bf16[16,128]{1,0:T(8,128)(2,1)} %get-tuple-element.8), slice={[0:8], [0:128]} | slice | bytes 4096 | tf_op jit(solution)/shard_map/slice | solution.py:606
  69.2 1.3 %copy.16 = bf16[32,256]{1,0:T(8,128)(2,1)} copy(bf16[32,256]{1,0:T(8,128)(2,1)} %get-tuple-element.12) | data formatting | bytes 32768

commit v3 on v2

--- a/solution.py
+++ b/solution.py
@@ -2,6 +2,7 @@
 
 import jax
 import jax.numpy as jnp
+import numpy as np
 from jax import lax
 from jax.experimental import pallas as pl
 from jax.experimental.pallas import tpu as pltpu
@@ -84,12 +85,10 @@
     w8,
     s9,
     r9,
-    s_out,
     load_sems,
     send_sems,
     recv_sems,
     query_sems,
-    out_sems,
 ):
     plane = row_size * kv_size
     tp = lax.axis_index("tp")
@@ -199,10 +198,12 @@
         2: r3.at[pl.ds(0, kv_size - 1)],
         3: r4.at[pl.ds(0, kv_size - 1)],
         4: r5.at[pl.ds(0, (plane - 1) * 8)],
-        5: r6.at[pl.ds(0, tp_size - 1)],
+        5: r6.at[0, pl.ds(0, tp_size - 1)],
+        11: r6.at[1, pl.ds(0, tp_size - 1)],
         6: r7.at[pl.ds(0, plane - 1)],
         7: r8.at[pl.ds(0, plane - 1)],
-        8: r9.at[pl.ds(0, tp_size - 1)],
+        8: r9.at[0, pl.ds(0, tp_size - 1)],
+        12: r9.at[1, pl.ds(0, tp_size - 1)],
     }
 
     def drain():
@@ -404,10 +405,8 @@
     def _():
         whole(10, rp).wait_recv()
 
-    keys_out = pltpu.make_async_copy(rp.at[0], new_keys, out_sems.at[0])
-    values_out = pltpu.make_async_copy(rp.at[1], new_values, out_sems.at[1])
-    keys_out.start()
-    values_out.start()
+    new_keys[...] = rp[0][:slots]
+    new_values[...] = rp[1][:slots]
     this_slot = iota((slots, HEAD), 0) == kv
     fresh_key = jnp.sum(
         jnp.where(this_slot, rp[0].astype(F32)[:slots], 0.0), axis=0, keepdims=True
@@ -442,35 +441,67 @@
     )
     projected = jnp.dot(mixed_all, out_v[...], preferred_element_type=F32)
 
+    half = seqs // 2
+    half_rows = row_size // 2
+    my_block = row // half_rows
+
     projected = projected.astype(BF16)
-    s6[...] = projected
-    r6[tp] = projected
-    send_tp(5, s6, r6.at[tp])
+    for block, phase in enumerate((5, 11)):
+        part = projected[block * half : (block + 1) * half]
+        s6[block] = part
+        r6[block, tp] = part
+        send_tp(phase, s6.at[block], r6.at[block, tp])
     need("ffn", "gate", "up")
-    arrived(5)
-    projected = r6[0].astype(F32)
-    for source in range(1, tp_size):
-        projected = projected + r6[source].astype(F32)
-    stream_two = (stream + projected).astype(BF16).astype(F32)
-    square_column = jnp.broadcast_to(
-        jnp.sum(stream_two * stream_two, axis=1, keepdims=True), (seqs, HEAD)
-    )
-    scaled = (stream_two * ffn_gain[...].astype(F32).reshape(1, width)).astype(BF16)
-
-    gate = jnp.dot(scaled, gate_v[...], preferred_element_type=F32)
-    up = jnp.dot(scaled, up_v[...], preferred_element_type=F32)
-    chunks = gate.shape[1] // HEAD
-    for part in range(chunks):
-        w7[pl.ds(part, seqs, stride=32), :] = gate[:, part * HEAD : (part + 1) * HEAD]
-        w7[pl.ds(part + 16, seqs, stride=32), :] = up[:, part * HEAD : (part + 1) * HEAD]
-    blank = jnp.zeros((seqs, HEAD), F32)
-    high = square_column.astype(BF16).astype(F32)
-    w7[pl.ds(14, seqs, stride=32), :] = high
-    w7[pl.ds(15, seqs, stride=32), :] = square_column - high
-    w7[pl.ds(30, seqs, stride=32), :] = blank
-    w7[pl.ds(31, seqs, stride=32), :] = blank
-    s7[...] = w7[...].astype(BF16)
-    send_plane(6, lambda other: s7.at[pl.ds(pl.multiple_of(other * 32, 32), 32), :], r7.at[me])
+    ffn = ffn_gain[...].astype(F32).reshape(1, width)
+    blank = jnp.zeros((half, HEAD), F32)
+    chunks = gate_v.shape[1] // HEAD
+    streams = []
+    for block, phase in enumerate((5, 11)):
+        arrived(phase)
+        total = r6[block, 0].astype(F32)
+        for source in range(1, tp_size):
+            total = total + r6[block, source].astype(F32)
+        rows = (stream[block * half : (block + 1) * half] + total).astype(BF16).astype(F32)
+        streams.append(rows)
+        square_column = jnp.broadcast_to(
+            jnp.sum(rows * rows, axis=1, keepdims=True), (half, HEAD)
+        )
+        scaled = (rows * ffn).astype(BF16)
+
+        gate = jnp.dot(scaled, gate_v[...], preferred_element_type=F32)
+        up = jnp.dot(scaled, up_v[...], preferred_element_type=F32)
+        base = block * half * 32
+        for part in range(chunks):
+            columns = slice(part * HEAD, (part + 1) * HEAD)
+            w7[pl.ds(base + part, half, stride=32), :] = gate[:, columns]
+            w7[pl.ds(base + part + 16, half, stride=32), :] = up[:, columns]
+        high = square_column.astype(BF16).astype(F32)
+        w7[pl.ds(base + 14, half, stride=32), :] = high
+        w7[pl.ds(base + 15, half, stride=32), :] = square_column - high
+        w7[pl.ds(base + 30, half, stride=32), :] = blank
+        w7[pl.ds(base + 31, half, stride=32), :] = blank
+        s7[base : base + half * 32, :] = w7[base : base + half * 32, :].astype(BF16)
+
+        def send_partial(index, carry, block=block):
+            other_row = block * half_rows + lax.rem(index, half_rows)
+            other_kv = lax.rem(kv + far_first(index // half_rows, kv_size), kv_size)
+            other = other_row * kv_size + other_kv
+
+            @pl.when(other != me)
+            def _():
+                pltpu.make_async_remote_copy(
+                    src_ref=s7.at[pl.ds(pl.multiple_of(other * 32, 32), 32), :],
+                    dst_ref=r7.at[me],
+                    send_sem=send_sems.at[6],
+                    recv_sem=recv_sems.at[6],
+                    device_id={"row": other_row, "kv": other_kv},
+                    device_id_type=MESH,
+                ).start()
+
+            return carry
+
+        lax.fori_loop(0, half, send_partial, 0)
+    sent.append(6)
     r7[me] = s7[pl.ds(pl.multiple_of(me * 32, 32), 32), :]
     need("down")
     arrived(6)
@@ -482,30 +513,61 @@
 
     s8[...] = activated
     r8[me] = activated
-    send_plane(7, lambda other: s8, r8.at[me])
-    arrived(7)
-    w8[...] = r8[...].astype(F32).reshape(w8.shape)
-    active_all = jnp.concatenate(
-        [w8[pl.ds(part, seqs, stride=16), :].astype(BF16) for part in range(chunks)], axis=1
-    )
-    down = jnp.dot(active_all, down_v[...], preferred_element_type=F32)
-
-    down = down.astype(BF16)
-    s9[...] = down
-    r9[tp] = down
-    send_tp(8, s9, r9.at[tp])
-    arrived(8)
-    down = r9[0].astype(F32)
-    for source in range(1, tp_size):
-        down = down + r9[source].astype(F32)
-    result = (stream_two + down).astype(BF16)
-    s_out[...] = jnp.dot(to_seqs, result, preferred_element_type=F32).astype(BF16)
-    layer_copy = pltpu.make_async_copy(s_out, layer_out, out_sems.at[2])
-    layer_copy.start()
-    keys_out.wait()
-    values_out.wait()
-    layer_copy.wait()
+    def share_activated(index, carry):
+        other_row, other_kv = plane_partner(index)
+        pltpu.make_async_remote_copy(
+            src_ref=s8,
+            dst_ref=r8.at[me],
+            send_sem=send_sems.at[7],
+            recv_sem=recv_sems.at[7 + 6 * my_block],
+            device_id={"row": other_row, "kv": other_kv},
+            device_id_type=MESH,
+        ).start()
+        return carry
+
+    lax.fori_loop(0, plane - 1, share_activated, 0)
+    sent.append(7)
+    for block, phase in enumerate((8, 12)):
+
+        @pl.when(my_block == block)
+        def _(block=block):
+            whole(7 + 6 * block, r8.at[pl.ds(0, half - 1)]).wait_recv()
+
+        @pl.when(my_block != block)
+        def _(block=block):
+            whole(7 + 6 * block, r8.at[pl.ds(0, half)]).wait_recv()
+
+        w8[...] = r8[block * half : (block + 1) * half].astype(F32).reshape(w8.shape)
+        active = jnp.concatenate(
+            [w8[pl.ds(part, half, stride=16), :].astype(BF16) for part in range(chunks)], axis=1
+        )
+        down = jnp.dot(active, down_v[...], preferred_element_type=F32).astype(BF16)
+
+        s9[block] = down
+        r9[block, tp] = down
+        send_tp(phase, s9.at[block], r9.at[block, tp])
+    results = []
+    for block, phase in enumerate((8, 12)):
+        arrived(phase)
+        total = r9[block, 0].astype(F32)
+        for source in range(1, tp_size):
+            total = total + r9[block, source].astype(F32)
+        results.append((streams[block] + total).astype(BF16))
+    result = jnp.concatenate(results, axis=0)
+    layer_out[...] = jnp.dot(to_seqs, result, preferred_element_type=F32).astype(BF16)
     drain()
+
+
+def hand_out(result, keys, values, layer_out, new_keys, new_values, sems):
+    copies = [
+        pltpu.make_async_copy(result, layer_out, sems.at[0]),
+        pltpu.make_async_copy(keys, new_keys, sems.at[1]),
+        pltpu.make_async_copy(values, new_values, sems.at[2]),
+    ]
+    for copy in copies:
+        copy.start()
+    for copy in copies:
+        copy.wait()
 
 
 def local(
@@ -525,10 +587,10 @@
 ):
     tp_size, row_size, kv_size = sizes
     seqs, width = tokens.shape
-    half = HEAD // 2
-    pair = lax.rem(jnp.arange(HEAD, dtype=jnp.int32), half).astype(F32)
-    frequency = (ROPE_BASE ** (-(pair * 2.0 / HEAD))).reshape(1, HEAD)
+    pair = np.arange(HEAD) % (HEAD // 2)
+    frequency = (ROPE_BASE ** (-2.0 * pair / HEAD)).astype(np.float32).reshape(1, HEAD)
     plane = row_size * kv_size
+    vmem = pl.BlockSpec(memory_space=pltpu.VMEM)
     hbm = pl.BlockSpec(memory_space=pltpu.HBM)
     scratch = [
         pltpu.VMEM((1, HEAD), F32),
@@ -558,52 +620,65 @@
         pltpu.VMEM((kv_size, 16, HEAD), F32),
         pltpu.VMEM((8, HEAD), F32),
         pltpu.VMEM((plane * 8, HEAD), F32),
-        pltpu.VMEM((seqs, width), BF16),
-        pltpu.VMEM((tp_size, seqs, width), BF16),
+        pltpu.VMEM((2, seqs // 2, width), BF16),
+        pltpu.VMEM((2, tp_size, seqs // 2, width), BF16),
         pltpu.VMEM((plane * 32, HEAD), F32),
         pltpu.VMEM((plane * 32, HEAD), BF16),
         pltpu.VMEM((plane, 32, HEAD), BF16),
         pltpu.VMEM((16, HEAD), BF16),
         pltpu.VMEM((plane, 16, HEAD), BF16),
-        pltpu.VMEM((plane * 16, HEAD), F32),
-        pltpu.VMEM((seqs, width), BF16),
-        pltpu.VMEM((tp_size, seqs, width), BF16),
-        pltpu.VMEM((seqs, width), BF16),
+        pltpu.VMEM((plane * 8, HEAD), F32),
+        pltpu.VMEM((2, seqs // 2, width), BF16),
+        pltpu.VMEM((2, tp_size, seqs // 2, width), BF16),
         pltpu.SemaphoreType.DMA((13,)),
-        pltpu.SemaphoreType.DMA((11,)),
-        pltpu.SemaphoreType.DMA((11,)),
+        pltpu.SemaphoreType.DMA((14,)),
+        pltpu.SemaphoreType.DMA((14,)),
         pltpu.SemaphoreType.DMA((kv_size,)),
-        pltpu.SemaphoreType.DMA((3,)),
     ]
     result, keys, values = pl.pallas_call(
         functools.partial(kernel, tp_size, row_size, kv_size),
         out_shape=(
             jax.ShapeDtypeStruct((seqs, width), BF16),
-            jax.ShapeDtypeStruct((16, HEAD), BF16),
-            jax.ShapeDtypeStruct((16, HEAD), BF16),
+            jax.ShapeDtypeStruct((kv_size, HEAD), BF16),
+            jax.ShapeDtypeStruct((kv_size, HEAD), BF16),
         ),
         in_specs=[hbm] * 13,
-        out_specs=(hbm, hbm, hbm),
+        out_specs=(vmem, vmem, vmem),
         scratch_shapes=scratch,
         compiler_params=pltpu.CompilerParams(
-            collective_id=0, has_side_effects=True, vmem_limit_bytes=56 * 1024 * 1024
+            collective_id=0, has_side_effects=True, vmem_limit_bytes=24 * 1024 * 1024
         ),
     )(
-        frequency,
-        pool_seq,
-        cache_len,
-        tokens,
-        attn_gain,
-        ffn_gain,
-        w_qkv,
-        w_out,
-        w_gate,
-        w_up,
-        w_down,
-        cache_keys,
-        cache_values,
+        *(
+            pltpu.with_memory_space_constraint(part, pltpu.HBM)
+            for part in (
+                frequency,
+                pool_seq,
+                cache_len,
+                tokens,
+                attn_gain,
+                ffn_gain,
+                w_qkv,
+                w_out,
+                w_gate,
+                w_up,
+                w_down,
+                cache_keys,
+                cache_values,
+            )
+        )
     )
-    return result, keys[:kv_size], values[:kv_size]
+    return pl.pallas_call(
+        hand_out,
+        out_shape=(
+            jax.ShapeDtypeStruct((seqs, width), BF16),
+            jax.ShapeDtypeStruct((kv_size, HEAD), BF16),
+            jax.ShapeDtypeStruct((kv_size, HEAD), BF16),
+        ),
+        in_specs=[vmem] * 3,
+        out_specs=(hbm, hbm, hbm),
+        scratch_shapes=[pltpu.SemaphoreType.DMA((3,))],
+    )(*(pltpu.with_memory_space_constraint(part, pltpu.VMEM) for part in (result, keys, values)))
 
 
 def solution(mesh):

time: 70.8 us -> 65.9 us (0.931)
  local copies, waits for them, and re-layouts: 3.8 us -> 0 us
    slice x2 -> x0, local copies, waits for them, and re-layouts: 2.48 us -> none  [local(): return (result, keys[:kv_size], values[:kv_size])]
    unnamed x1 -> x0, local copies, waits for them, and re-layouts: 1.32 us -> none
    pallas_call x1, Pallas kernels: 65.6 us -> 64.6 us  [local(): pl.pallas_call(functools.partial(kernel, tp_size, row_size, kv_size), out...]
where the time goes in v3:
time: 65.9 us; the launch traced here: 65.8 us
  Pallas kernels  65.2 us (99%)
    pallas_call x1, Pallas kernels, local(): pl.pallas_call(functools.partial(kernel, tp_size, row_size, kv_size), out...  64.6 us

profile of v3, /device:TPU:1, one launch (start us, length us, event | category | flops | bytes accessed | tf_op | source)
XLA Modules:
  0.0 65.8 jit_solution(2293395477114994608)
XLA Ops:
  0.6 64.6 %shard_map.148 = (bf16[32,256]{1,0:T(8,128)(2,1)S(1)}, bf16[8,128]{1,0:T(8,128)(2,1)S(1)}, bf16[8,128]{1,0:T(8,128)(2,1)S(1)}) custom-call(f32[1,128]{1,0:T(1,128)} %constant.2.clone.frequency_hbm, s32[32]{0:T(128)} %pool_hbm.1, s32[32]{0:T(128)} %len_hbm.1, bf16[32,256]{1,0:T(8,128)(2,1)} %tokens_hbm.1, bf16[256]{0:T(256)(128)(2,1)} %attn_hbm.1, ...), custom_call_target="tpu_custom_call" | custom-call | tf_op jit(solution)/shard_map/pallas_call | solution.py:638
  65.2 0.6 shard_map.149

commit v4 on v3

--- a/solution.py
+++ b/solution.py
@@ -196,8 +196,8 @@
         0: r1.at[pl.ds(0, plane - 1)],
         1: r2.at[pl.ds(0, plane - 1)],
         2: r3.at[pl.ds(0, kv_size - 1)],
-        3: r4.at[pl.ds(0, kv_size - 1)],
-        4: r5.at[pl.ds(0, (plane - 1) * 8)],
+        3: r4.at[pl.ds(0, 2 * (kv_size - 1))],
+        4: r5.at[pl.ds(0, plane // 2 - 1)],
         5: r6.at[0, pl.ds(0, tp_size - 1)],
         11: r6.at[1, pl.ds(0, tp_size - 1)],
         6: r7.at[pl.ds(0, plane - 1)],
@@ -231,14 +231,21 @@
     width = tokens.shape[1]
     need("pool", "tokens")
     holder = jnp.zeros((seqs, seqs), jnp.int32)
+    for slot in range(seqs):
+        holder = jnp.where(iota((seqs, seqs), 0) == slot, pool_smem[slot], holder)
+    to_slots = (holder == iota((seqs, seqs), 1)).astype(BF16)
+    stream = jnp.dot(to_slots, tokens[...], preferred_element_type=F32)
+    quarter = kv_size // 2
+    holder = jnp.zeros((seqs, seqs), jnp.int32)
     held = jnp.zeros((seqs, seqs), jnp.int32)
-    for slot in range(seqs):
-        seq = pool_smem[slot]
-        holder = jnp.where(iota((seqs, seqs), 0) == slot, seq, holder)
-        held = jnp.where(iota((seqs, seqs), 1) == slot, seq, held)
-    to_slots = (holder == iota((seqs, seqs), 1)).astype(BF16)
+    for index in range(seqs):
+        group, place = index // kv_size, index % kv_size
+        seq = pool_smem[group * kv_size + place // 2 + quarter * (place % 2)]
+        holder = jnp.where(iota((seqs, seqs), 0) == index, seq, holder)
+        held = jnp.where(iota((seqs, seqs), 1) == index, seq, held)
+    to_pairs = (holder == iota((seqs, seqs), 1)).astype(BF16)
     to_seqs = (held == iota((seqs, seqs), 0)).astype(BF16)
-    stream = jnp.dot(to_slots, tokens[...], preferred_element_type=F32)
+    stream_pairs = jnp.dot(to_pairs, tokens[...], preferred_element_type=F32)
 
     wide = iota((seqs, HEAD), 0) == iota((seqs, HEAD), 1)
 
@@ -356,7 +363,7 @@
     score_scale = HEAD ** (-0.5)
     position = kv * block + iota((GROUP, block), 1)
     lane = iota((GROUP, HEAD), 1)
-    for group in ((0,), (1, 7), (2, 6), (4,), (3, 5)):
+    for group in ((0,), (1, 7), (2, 6), (4, 3, 5)):
         at = [lax.rem(kv + offset, kv_size) for offset in group]
         for offset, slot in zip(group, at):
             if offset:
@@ -374,27 +381,28 @@
         results = []
         for slot, score in zip(at, scores):
             limit = len_smem[pool_smem[row * slots + slot]]
-            allowed = position < limit
-            peak = jnp.max(jnp.where(allowed, score, FLOOR), axis=1, keepdims=True)
-            weights = jnp.where(allowed, jnp.exp(score - peak), 0.0)
+            score = jnp.where(position < limit, score, FLOOR)
+            peak = jnp.maximum(jnp.max(score, axis=1, keepdims=True), 0.1 * FLOOR)
+            weights = jnp.exp(score - peak)
             total = jnp.sum(weights, axis=1, keepdims=True)
             product = jnp.dot(weights.astype(BF16), values_v[slot], preferred_element_type=F32)
             results.append((product, jnp.where(lane == 0, peak, total)))
         for offset, slot, (product, stats) in zip(group, at, results):
-            if offset == 0:
-                r4[kv, :GROUP] = product
-                r4[kv, GROUP:] = stats
-            else:
-                s4[slot, :GROUP] = product
-                s4[slot, GROUP:] = stats
-                pltpu.make_async_remote_copy(
-                    src_ref=s4.at[slot],
-                    dst_ref=r4.at[kv],
-                    send_sem=send_sems.at[3],
-                    recv_sem=recv_sems.at[3],
-                    device_id={"kv": slot},
-                    device_id_type=MESH,
-                ).start()
+            place = slot // quarter * kv_size + kv
+            s4[slot, :GROUP] = product
+            s4[slot, GROUP:] = stats
+            for target in (offset, (offset + quarter) % kv_size):
+                if target == 0:
+                    r4[place] = s4[slot]
+                else:
+                    pltpu.make_async_remote_copy(
+                        src_ref=s4.at[slot],
+                        dst_ref=r4.at[place],
+                        send_sem=send_sems.at[3],
+                        recv_sem=recv_sems.at[3],
+                        device_id={"kv": lax.rem(kv + target, kv_size)},
+                        device_id_type=MESH,
+                    ).start()
     sent.append(3)
 
     @pl.when(owns_fresh)
@@ -407,37 +415,59 @@
 
     new_keys[...] = rp[0][:slots]
     new_values[...] = rp[1][:slots]
-    this_slot = iota((slots, HEAD), 0) == kv
-    fresh_key = jnp.sum(
-        jnp.where(this_slot, rp[0].astype(F32)[:slots], 0.0), axis=0, keepdims=True
-    )
-    fresh_value = jnp.sum(
-        jnp.where(this_slot, rp[1].astype(F32)[:slots], 0.0), axis=0, keepdims=True
-    )
-    fresh_query = mine.astype(F32)[:GROUP]
-    fresh_score = jnp.sum(fresh_query * fresh_key, axis=1, keepdims=True) * score_scale
+    fresh_keys = rp[0].astype(F32)
+    fresh_values = rp[1].astype(F32)
+    fresh = []
+    for which in range(2):
+        slot = lax.rem(kv, quarter) + quarter * which
+        this_slot = iota((16, HEAD), 0) == slot
+        fresh_key = jnp.sum(jnp.where(this_slot, fresh_keys, 0.0), axis=0, keepdims=True)
+        fresh_value = jnp.sum(jnp.where(this_slot, fresh_values, 0.0), axis=0, keepdims=True)
+        fresh_query = r3[slot].astype(F32)[:GROUP]
+        fresh_score = jnp.sum(fresh_query * fresh_key, axis=1, keepdims=True) * score_scale
+        fresh.append((fresh_score, fresh_value))
     arrived(3)
-    parts = r4[...]
-    peaks = [parts[source, GROUP:, 0:1] for source in range(slots)]
-    joint = fresh_score
-    for peak in peaks:
-        joint = jnp.maximum(joint, peak)
-    fresh_weight = jnp.exp(fresh_score - joint)
-    total = fresh_weight
-    numer = fresh_weight.astype(BF16).astype(F32) * fresh_value
-    for source in range(slots):
-        fade = jnp.exp(peaks[source] - joint)
-        total = total + parts[source, GROUP:, 1:2] * fade
-        numer = numer + parts[source, :GROUP] * fade
-    mixed = numer / total
-
+    mixed = []
+    for which, (fresh_score, fresh_value) in enumerate(fresh):
+        parts = r4[which * kv_size : (which + 1) * kv_size]
+        peaks = [parts[source, GROUP:, 0:1] for source in range(slots)]
+        joint = fresh_score
+        for peak in peaks:
+            joint = jnp.maximum(joint, peak)
+        fresh_weight = jnp.exp(fresh_score - joint)
+        total = fresh_weight
+        numer = fresh_weight.astype(BF16).astype(F32) * fresh_value
+        for source in range(slots):
+            fade = jnp.exp(peaks[source] - joint)
+            total = total + parts[source, GROUP:, 1:2] * fade
+            numer = numer + parts[source, :GROUP] * fade
+        mixed.append(numer / total)
+    mixed = jnp.concatenate(mixed, axis=0).astype(BF16)
+
+    pair = row * quarter + lax.rem(kv, quarter)
     s5[...] = mixed
-    r5[pl.ds(pl.multiple_of(me * 8, 8), 8), :] = mixed
-    send_plane(4, lambda other: s5, r5.at[pl.ds(pl.multiple_of(me * 8, 8), 8), :])
+    r5[pair] = mixed
+    for kv_step, row_step in (
+        (2, 2), (2, 1), (2, 3), (7, 2), (1, 2), (2, 0), (7, 1), (7, 3),
+        (1, 1), (1, 3), (0, 2), (7, 0), (1, 0), (0, 1), (0, 3),
+    ):
+        pltpu.make_async_remote_copy(
+            src_ref=s5,
+            dst_ref=r5.at[pair],
+            send_sem=send_sems.at[4],
+            recv_sem=recv_sems.at[4],
+            device_id={
+                "row": lax.rem(row + row_step, row_size),
+                "kv": lax.rem(kv + kv_step, kv_size),
+            },
+            device_id_type=MESH,
+        ).start()
+    sent.append(4)
     need("out")
     arrived(4)
+    w8[...] = r5[...].astype(F32).reshape(w8.shape)
     mixed_all = jnp.concatenate(
-        [r5[pl.ds(head, seqs, stride=8), :].astype(BF16) for head in range(GROUP)], axis=1
+        [w8[pl.ds(head, seqs, stride=8), :].astype(BF16) for head in range(GROUP)], axis=1
     )
     projected = jnp.dot(mixed_all, out_v[...], preferred_element_type=F32)
 
@@ -461,7 +491,7 @@
         total = r6[block, 0].astype(F32)
         for source in range(1, tp_size):
             total = total + r6[block, source].astype(F32)
-        rows = (stream[block * half : (block + 1) * half] + total).astype(BF16).astype(F32)
+        rows = (stream_pairs[block * half : (block + 1) * half] + total).astype(BF16).astype(F32)
         streams.append(rows)
         square_column = jnp.broadcast_to(
             jnp.sum(rows * rows, axis=1, keepdims=True), (half, HEAD)
@@ -617,9 +647,9 @@
         pltpu.VMEM((16, HEAD), BF16),
         pltpu.VMEM((2, 16, HEAD), BF16),
         pltpu.VMEM((kv_size, 16, HEAD), F32),
-        pltpu.VMEM((kv_size, 16, HEAD), F32),
-        pltpu.VMEM((8, HEAD), F32),
-        pltpu.VMEM((plane * 8, HEAD), F32),
+        pltpu.VMEM((2 * kv_size, 16, HEAD), F32),
+        pltpu.VMEM((16, HEAD), BF16),
+        pltpu.VMEM((plane // 2, 16, HEAD), BF16),
         pltpu.VMEM((2, seqs // 2, width), BF16),
         pltpu.VMEM((2, tp_size, seqs // 2, width), BF16),
         pltpu.VMEM((plane * 32, HEAD), F32),

time: 65.9 us -> 64 us (0.971)
  Pallas kernels: 65.2 us -> 63.3 us
    pallas_call x1, Pallas kernels: 64.6 us -> 62.6 us  [local(): pl.pallas_call(functools.partial(kernel, tp_size, row_size, kv_size), out...]
where the time goes in v4:
time: 64 us; the launch traced here: 63.9 us
  Pallas kernels  63.3 us (99%)
  between operations  0.64 us (1%)
    pallas_call x1, Pallas kernels, local(): pl.pallas_call(functools.partial(kernel, tp_size, row_size, kv_size), out...  62.6 us

profile of v4, /device:TPU:1, one launch (start us, length us, event | category | flops | bytes accessed | tf_op | source)
XLA Modules:
  0.0 63.9 jit_solution(9400452573808918657)
XLA Ops:
  0.6 62.6 %shard_map.148 = (bf16[32,256]{1,0:T(8,128)(2,1)S(1)}, bf16[8,128]{1,0:T(8,128)(2,1)S(1)}, bf16[8,128]{1,0:T(8,128)(2,1)S(1)}) custom-call(f32[1,128]{1,0:T(1,128)} %constant.2.clone.frequency_hbm, s32[32]{0:T(128)} %pool_hbm.1, s32[32]{0:T(128)} %len_hbm.1, bf16[32,256]{1,0:T(8,128)(2,1)} %tokens_hbm.1, bf16[256]{0:T(256)(128)(2,1)} %attn_hbm.1, ...), custom_call_target="tpu_custom_call" | custom-call | tf_op jit(solution)/shard_map/pallas_call | solution.py:668
  63.3 0.6 shard_map.149

commit v5 on v4

--- a/solution.py
+++ b/solution.py
@@ -61,6 +61,7 @@
     down_v,
     keys_v,
     values_v,
+    turned_keys,
     s1,
     r1,
     s2,
@@ -213,11 +214,11 @@
         if 1 in sent:
             @pl.when(owns_fresh)
             def _():
-                whole(9, rf.at[pl.ds(0, 2 * row_size - 1)]).wait_send()
+                whole(9, rf.at[pl.ds(0, row_size - 1)]).wait_send()
 
             @pl.when(jnp.logical_not(owns_fresh))
             def _():
-                whole(9, rf.at[pl.ds(0, 2 * row_size)]).wait_send()
+                whole(9, rf.at[pl.ds(0, row_size)]).wait_send()
 
         if 2 in sent:
             @pl.when(owns_fresh)
@@ -275,37 +276,47 @@
     united = jnp.dot(normed, qkv_v[...], preferred_element_type=F32)
     for part in range(GROUP):
         s2[pl.ds(part, seqs, stride=GROUP), :] = united[:, part * HEAD : (part + 1) * HEAD]
-    for part in range(2):
-        sf[part] = united[:, (GROUP + part) * HEAD : (GROUP + part + 1) * HEAD]
+    fresh = united[:, GROUP * HEAD :].astype(BF16).astype(F32)
+    for group in range(row_size):
+        rows = slice(group * kv_size, (group + 1) * kv_size)
+        sf[group] = jnp.concatenate(
+            [fresh[rows, :HEAD], fresh[rows, HEAD:]], axis=0
+        ).astype(BF16)
     send_plane(1, lambda other: s2.at[pl.ds(pl.multiple_of(other * 8, 8), 8), :], r2.at[me])
     r2[me] = s2[pl.ds(pl.multiple_of(me * 8, 8), 8), :]
 
     def send_fresh(index, carry):
-        owner_row, part = index // 2, lax.rem(index, 2)
-        owner_kv = index
-
-        @pl.when(jnp.logical_not((owner_row == row) & (owner_kv == kv)))
+        @pl.when(jnp.logical_not((index == row) & (2 * index == kv)))
         def _():
             pltpu.make_async_remote_copy(
-                src_ref=sf.at[part, pl.ds(pl.multiple_of(owner_row * kv_size, 8), kv_size), :],
+                src_ref=sf.at[index],
                 dst_ref=rf.at[me],
                 send_sem=send_sems.at[9],
                 recv_sem=recv_sems.at[9],
-                device_id={"row": owner_row, "kv": owner_kv},
+                device_id={"row": index, "kv": 2 * index},
                 device_id_type=MESH,
             ).start()
 
         return carry
 
-    lax.fori_loop(0, 2 * row_size, send_fresh, 0)
-    owns_fresh = kv // 2 == row
-    fresh_part = lax.rem(kv, 2)
+    lax.fori_loop(0, row_size, send_fresh, 0)
+    owns_fresh = kv == 2 * row
     lane_sign = jnp.where(iota((1, HEAD), 1) < HEAD // 2, -1.0, 1.0)
     angle = len_smem[pool_smem[me]].astype(F32) * frequency[...]
     cosine = jnp.cos(angle)
     sine = jnp.sin(angle) * lane_sign
     slots = kv_size
-    limits = [len_smem[pool_smem[row * slots + slot]] for slot in range(slots)]
+    column = jnp.zeros((2 * slots, HEAD), jnp.int32)
+    for slot in range(slots):
+        limit = len_smem[pool_smem[row * slots + slot]]
+        column = jnp.where(iota((2 * slots, HEAD), 0) == slot, limit, column)
+    angles = column.astype(F32) * frequency[...]
+    turned = iota((2 * slots, HEAD), 0) < slots
+    cosines = jnp.where(turned, jnp.cos(angles), 1.0)
+    sines = jnp.where(turned, jnp.sin(angles) * lane_sign, 0.0)
+    need("keys")
+    for slot in range(slots):
+        turned_keys[slot] = keys_v[slot].T
     arrived(1)
     mine = jnp.sum(r2[...], axis=0)
     mine = mine * cosine + pltpu.roll(mine, HEAD // 2, 1) * sine
@@ -331,24 +342,17 @@
 
     @pl.when(owns_fresh)
     def _():
-        rf[me] = sf[fresh_part, pl.ds(pl.multiple_of(row * kv_size, 8), kv_size), :]
-        column = jnp.zeros((slots, HEAD), jnp.int32)
-        for slot in range(slots):
-            column = jnp.where(iota((slots, HEAD), 0) == slot, limits[slot], column)
-        angles = column.astype(F32) * frequency[...]
-        cosines = jnp.where(fresh_part == 0, jnp.cos(angles), 1.0)
-        sines = jnp.where(fresh_part == 0, jnp.sin(angles) * lane_sign, 0.0)
+        rf[me] = sf[row]
         whole(9, rf.at[pl.ds(0, plane - 1)]).wait_recv()
-        fresh = jnp.sum(rf[...], axis=0)
+        fresh = jnp.sum(rf[...].astype(F32), axis=0)
         fresh = fresh * cosines + pltpu.roll(fresh, HEAD // 2, 1) * sines
-        fresh = jnp.concatenate([fresh, jnp.zeros_like(fresh)], axis=0).astype(BF16)
-        sp[...] = fresh
-        rp[fresh_part] = fresh
+        sp[...] = fresh.astype(BF16)
+        rp[...] = fresh.astype(BF16)
 
         def share(step, carry):
             pltpu.make_async_remote_copy(
                 src_ref=sp,
-                dst_ref=rp.at[fresh_part],
+                dst_ref=rp,
                 send_sem=send_sems.at[10],
                 recv_sem=recv_sems.at[10],
                 device_id={"kv": lax.rem(kv + step, kv_size)},
@@ -358,12 +362,12 @@
 
         lax.fori_loop(1, kv_size, share, 0)
 
-    need("keys", "values")
+    need("values")
     block = keys_v.shape[1]
     score_scale = HEAD ** (-0.5)
     position = kv * block + iota((GROUP, block), 1)
     lane = iota((GROUP, HEAD), 1)
-    for group in ((0,), (1, 7), (2, 6), (4, 3, 5)):
+    for group in ((0,), (1, 7), (2, 6, 3, 5), (4,)):
         at = [lax.rem(kv + offset, kv_size) for offset in group]
         for offset, slot in zip(group, at):
             if offset:
@@ -371,8 +375,8 @@
         scores = [
             lax.dot_general(
                 r3[slot, :GROUP, :],
-                keys_v[slot],
-                (((1,), (1,)), ((), ())),
+                turned_keys[slot],
+                (((1,), (0,)), ((), ())),
                 preferred_element_type=F32,
             )
             * score_scale
@@ -391,7 +395,7 @@
             place = slot // quarter * kv_size + kv
             s4[slot, :GROUP] = product
             s4[slot, GROUP:] = stats
-            for target in (offset, (offset + quarter) % kv_size):
+            for target in ((offset + 2) % kv_size, (offset + 2 + quarter) % kv_size):
                 if target == 0:
                     r4[place] = s4[slot]
                 else:
@@ -405,22 +409,18 @@
                     ).start()
     sent.append(3)
 
-    @pl.when(owns_fresh)
-    def _():
-        whole(10, rp.at[0]).wait_recv()
-
     @pl.when(jnp.logical_not(owns_fresh))
     def _():
         whole(10, rp).wait_recv()
 
-    new_keys[...] = rp[0][:slots]
-    new_values[...] = rp[1][:slots]
-    fresh_keys = rp[0].astype(F32)
-    fresh_values = rp[1].astype(F32)
+    fresh = rp[...].astype(F32)
+    fresh_keys, fresh_values = fresh[:slots], fresh[slots:]
+    new_keys[...] = fresh_keys.astype(BF16)
+    new_values[...] = fresh_values.astype(BF16)
     fresh = []
     for which in range(2):
-        slot = lax.rem(kv, quarter) + quarter * which
-        this_slot = iota((16, HEAD), 0) == slot
+        slot = lax.rem(kv + 2, quarter) + quarter * which
+        this_slot = iota((slots, HEAD), 0) == slot
         fresh_key = jnp.sum(jnp.where(this_slot, fresh_keys, 0.0), axis=0, keepdims=True)
         fresh_value = jnp.sum(jnp.where(this_slot, fresh_values, 0.0), axis=0, keepdims=True)
         fresh_query = r3[slot].astype(F32)[:GROUP]
@@ -444,7 +444,7 @@
         mixed.append(numer / total)
     mixed = jnp.concatenate(mixed, axis=0).astype(BF16)
 
-    pair = row * quarter + lax.rem(kv, quarter)
+    pair = row * quarter + lax.rem(kv + 2, quarter)
     s5[...] = mixed
     r5[pair] = mixed
     for kv_step, row_step in (
@@ -636,16 +636,17 @@
         pltpu.VMEM(w_down.shape, BF16),
         pltpu.VMEM(cache_keys.shape, BF16),
         pltpu.VMEM(cache_values.shape, BF16),
+        pltpu.VMEM((kv_size, HEAD, cache_keys.shape[1]), BF16),
         pltpu.VMEM((1, 1, HEAD), F32),
         pltpu.VMEM((plane, 1, HEAD), F32),
         pltpu.VMEM((plane * 8, HEAD), F32),
         pltpu.VMEM((plane, 8, HEAD), F32),
-        pltpu.VMEM((2, plane, HEAD), F32),
-        pltpu.VMEM((plane, 8, HEAD), F32),
+        pltpu.VMEM((row_size, 16, HEAD), BF16),
+        pltpu.VMEM((plane, 16, HEAD), BF16),
         pltpu.VMEM((16, HEAD), BF16),
         pltpu.VMEM((kv_size, 16, HEAD), BF16),
         pltpu.VMEM((16, HEAD), BF16),
-        pltpu.VMEM((2, 16, HEAD), BF16),
+        pltpu.VMEM((16, HEAD), BF16),
         pltpu.VMEM((kv_size, 16, HEAD), F32),
         pltpu.VMEM((2 * kv_size, 16, HEAD), F32),
         pltpu.VMEM((16, HEAD), BF16),

time: 64 us -> 63.4 us (level)
  no operation moved by 1% of the time
where the time goes in v5:
time: 63.4 us; the launch traced here: 63.3 us
  Pallas kernels  62.7 us (99%)
  between operations  0.64 us (1%)
    pallas_call x1, Pallas kernels, local(): pl.pallas_call(functools.partial(kernel, tp_size, row_size, kv_size), out...  62 us

profile of v5, /device:TPU:1, one launch (start us, length us, event | category | flops | bytes accessed | tf_op | source)
XLA Modules:
  0.0 63.3 jit_solution(8102250414741311434)
XLA Ops:
  0.6 62.0 %shard_map.148 = (bf16[32,256]{1,0:T(8,128)(2,1)S(1)}, bf16[8,128]{1,0:T(8,128)(2,1)S(1)}, bf16[8,128]{1,0:T(8,128)(2,1)S(1)}) custom-call(f32[1,128]{1,0:T(1,128)} %constant.2.clone.frequency_hbm, s32[32]{0:T(128)} %pool_hbm.1, s32[32]{0:T(128)} %len_hbm.1, bf16[32,256]{1,0:T(8,128)(2,1)} %tokens_hbm.1, bf16[256]{0:T(256)(128)(2,1)} %attn_hbm.1, ...), custom_call_target="tpu_custom_call" | custom-call | tf_op jit(solution)/shard_map/pallas_call | solution.py:669
  62.7 0.6 %shard_map.149 = (bf16[32,256]{1,0:T(8,128)(2,1)}, bf16[8,128]{1,0:T(8,128)(2,1)}, bf16[8,128]{1,0:T(8,128)(2,1)}) custom-call(bf16[32,256]{1,0:T(8,128)(2,1)S(1)} %get-tuple-element.6.result, bf16[8,128]{1,0:T(8,128)(2,1)S(1)} %get-tuple-element.7.keys, bf16[8,128]{1,0:T(8,128)(2,1)S(1)} %get-tuple-element.8.values), custom_call_target="tpu_custom_call" | custom-call | tf_op jit(solution)/shard_map/pallas_call | solution.py:702

commit v6 on v5

--- a/solution.py
+++ b/solution.py
@@ -142,17 +142,14 @@
         )
     ):
         pending[name] = pltpu.make_async_copy(source, target, load_sems.at[index])
-        pending[name].start()
+        if index < 8:
+            pending[name].start()
 
     def need(*names):
         for name in names:
             pending.pop(name).wait()
 
-    sent = []
-
     def send_plane(phase, source, target):
-        sent.append(phase)
-
         def one(index, carry):
             other_row, other_kv = plane_partner(index)
             pltpu.make_async_remote_copy(
@@ -168,8 +165,6 @@
         lax.fori_loop(0, plane - 1, one, 0)
 
     def send_tp(phase, source, target):
-        sent.append(phase)
-
         def one(index, carry):
             pltpu.make_async_remote_copy(
                 src_ref=source,
@@ -207,23 +202,19 @@
         12: r9.at[1, pl.ds(0, tp_size - 1)],
     }
 
-    def drain():
-        for phase in sent:
+    def drain(*phases):
+        for phase in phases:
             whole(phase, others[phase]).wait_send()
 
-        if 1 in sent:
-            @pl.when(owns_fresh)
-            def _():
-                whole(9, rf.at[pl.ds(0, row_size - 1)]).wait_send()
-
-            @pl.when(jnp.logical_not(owns_fresh))
-            def _():
-                whole(9, rf.at[pl.ds(0, row_size)]).wait_send()
-
-        if 2 in sent:
-            @pl.when(owns_fresh)
-            def _():
-                whole(10, r3.at[pl.ds(0, kv_size - 1)]).wait_send()
+    def drain_fresh():
+        @pl.when(owns_fresh)
+        def _():
+            whole(9, rf.at[pl.ds(0, row_size - 1)]).wait_send()
+            whole(10, r3.at[pl.ds(0, kv_size - 1)]).wait_send()
+
+        @pl.when(jnp.logical_not(owns_fresh))
+        def _():
+            whole(9, rf.at[pl.ds(0, row_size)]).wait_send()
 
     def arrived(phase):
         whole(phase, others[phase]).wait_recv()
@@ -314,6 +305,8 @@
     turned = iota((2 * slots, HEAD), 0) < slots
     cosines = jnp.where(turned, jnp.cos(angles), 1.0)
     sines = jnp.where(turned, jnp.sin(angles) * lane_sign, 0.0)
+    for name in ("out", "ffn", "gate", "up", "down"):
+        pending[name].start()
     need("keys")
     for slot in range(slots):
         turned_keys[slot] = keys_v[slot].T
@@ -338,7 +331,6 @@
     for index in range(kv_size - 1):
         offset = (4, 3, 5, 2, 6, 1, 7)[index]
         query_copy(offset, kv, kv_size - offset).start()
-    sent.append(2)
 
     @pl.when(owns_fresh)
     def _():
@@ -407,7 +399,6 @@
                         device_id={"kv": lax.rem(kv + target, kv_size)},
                         device_id_type=MESH,
                     ).start()
-    sent.append(3)
 
     @pl.when(jnp.logical_not(owns_fresh))
     def _():
@@ -462,7 +453,6 @@
             },
             device_id_type=MESH,
         ).start()
-    sent.append(4)
     need("out")
     arrived(4)
     w8[...] = r5[...].astype(F32).reshape(w8.shape)
@@ -531,9 +521,10 @@
             return carry
 
         lax.fori_loop(0, half, send_partial, 0)
-    sent.append(6)
     r7[me] = s7[pl.ds(pl.multiple_of(me * 32, 32), 32), :]
     need("down")
+    drain(0, 1, 2, 3, 4)
+    drain_fresh()
     arrived(6)
     sums = jnp.sum(r7[...].astype(F32), axis=0)
     scale = lax.rsqrt((sums[14:15] + sums[15:16]) / D + EPSILON)
@@ -556,7 +547,7 @@
         return carry
 
     lax.fori_loop(0, plane - 1, share_activated, 0)
-    sent.append(7)
+    drain(5, 11, 6)
     for block, phase in enumerate((8, 12)):
 
         @pl.when(my_block == block)
@@ -585,7 +576,7 @@
         results.append((streams[block] + total).astype(BF16))
     result = jnp.concatenate(results, axis=0)
     layer_out[...] = jnp.dot(to_seqs, result, preferred_element_type=F32).astype(BF16)
-    drain()
+    drain(7, 8, 12)
 
 
 def hand_out(result, keys, values, layer_out, new_keys, new_values, sems):

time: 63.4 us -> 63.4 us (level)
  no operation moved by 1% of the time
where the time goes in v6:
time: 63.4 us; the launch traced here: 63.3 us
  Pallas kernels  62.7 us (99%)
  between operations  0.64 us (1%)
    pallas_call x1, Pallas kernels, local(): pl.pallas_call(functools.partial(kernel, tp_size, row_size, kv_size), out...  62 us

profile of v6, /device:TPU:1, one launch (start us, length us, event | category | flops | bytes accessed | tf_op | source)
XLA Modules:
  0.0 63.3 jit_solution(10985319990698251981)
XLA Ops:
  0.6 62.0 %shard_map.148 = (bf16[32,256]{1,0:T(8,128)(2,1)S(1)}, bf16[8,128]{1,0:T(8,128)(2,1)S(1)}, bf16[8,128]{1,0:T(8,128)(2,1)S(1)}) custom-call(f32[1,128]{1,0:T(1,128)} %constant.2.clone.frequency_hbm, s32[32]{0:T(128)} %pool_hbm.1, s32[32]{0:T(128)} %len_hbm.1, bf16[32,256]{1,0:T(8,128)(2,1)} %tokens_hbm.1, bf16[256]{0:T(256)(128)(2,1)} %attn_hbm.1, ...), custom_call_target="tpu_custom_call" | custom-call | tf_op jit(solution)/shard_map/pallas_call | solution.py:660
  62.7 0.6 %shard_map.149 = (bf16[32,256]{1,0:T(8,128)(2,1)}, bf16[8,128]{1,0:T(8,128)(2,1)}, bf16[8,128]{1,0:T(8,128)(2,1)}) custom-call(bf16[32,256]{1,0:T(8,128)(2,1)S(1)} %get-tuple-element.6.result, bf16[8,128]{1,0:T(8,128)(2,1)S(1)} %get-tuple-element.7.keys, bf16[8,128]{1,0:T(8,128)(2,1)S(1)} %get-tuple-element.8.values), custom_call_target="tpu_custom_call" | custom-call | tf_op jit(solution)/shard_map/pallas_call | solution.py:693
